TPU v7x, 128 devices: a whole 4x4x4 slice. The times are simulated.
128 devices in a mesh: row: 16 (over z, x_hi, core), col: 8 (over x_lo, y).
Axes of the slice: x: 4 (x_hi: 2, x_lo: 2; x = x_hi * 2 + x_lo), y: 4, z: 4, core: 2. Of those that a mesh axis runs over, the one named last changes fastest.
Arguments:
- codes: int32 [512, 512], P('row', 'col'), may hold values from 0 to 511
- starts: int32 [512], replicated, may hold values from 0 to 511, as said below
- embed: bfloat16 [512, 512], replicated, may hold values from -6 to 6
- gain_one: float32 [512], replicated, may hold values from 0.1 to 1.9
- row_qkv: bfloat16 [512, 1536], replicated, may hold values from -2 to 2
- row_out: bfloat16 [512, 512], replicated, may hold values from -0.25 to 0.25
- gain_two: float32 [512], replicated, may hold values from 0.1 to 1.9
- col_qkv: bfloat16 [512, 640], replicated, may hold values from -2 to 2
- col_out: bfloat16 [512, 512], replicated, may hold values from -0.25 to 0.25
- gain_three: float32 [512], replicated, may hold values from 0.1 to 1.9
- mlp_in: bfloat16 [512, 1024], replicated, may hold values from -0.25 to 0.25
- mlp_out: bfloat16 [1024, 512], replicated, may hold values from -0.1875 to 0.1875
- project: bfloat16 [512, 128], replicated, may hold values from -0.25 to 0.25
- conv_one: bfloat16 [3, 3, 128, 128], replicated, may hold values from -0.1875 to 0.1875
- conv_two: bfloat16 [3, 3, 128, 128], replicated, may hold values from -0.1875 to 0.1875
Outputs:
- block_out: float32 [512, 512, 512], P('row', 'col')
- image: float32 [1024, 1024, 128], P('row', 'col')
Inputs may be any that keep to these rules, and one draw needn't show every extreme that they name: starts[i] is at most i.
All inputs are finite; a program needn't handle non-finite values.
Results may differ from a plain program's by a relative error of at most 0.013.
The roundings to bfloat16 on the way count: a program that leaves them out, or rounds other values in their place, can miss the bound.
Values may be sent and summed in bfloat16 or wider, within the bound.
A program may use at most 192 MiB of HBM per device.

v0:
```python
import jax
import jax.numpy as jnp
from jax import lax
from jax.sharding import PartitionSpec as P

HEADS = 8


EPS = 1e-06
NEGATIVE = -1e30


def padded_2(block, sides, width):
    for axis, dim in sides:
        count = lax.axis_size(axis)
        forward = [(i, i + 1) for i in range(count - 1)]
        backward = [(target, source) for source, target in forward]
        low = lax.ppermute(
            lax.slice_in_dim(block, block.shape[dim] - width, None, axis=dim), axis, forward
        )
        high = lax.ppermute(lax.slice_in_dim(block, 0, width, axis=dim), axis, backward)
        block = jnp.concatenate([low, block, high], axis=dim)
    return block


def norm_round(values, norm_gain):
    scale = lax.rsqrt(jnp.mean(values * values, axis=-1, keepdims=True) + EPS)
    return (values * scale * norm_gain).astype(jnp.bfloat16)


def matmul(left, right):
    return jnp.einsum("...i,ij->...j", left, right, preferred_element_type=jnp.float32)


def softmax_round(scores, visible):
    scores = jnp.where(visible, scores, NEGATIVE)
    top = jnp.max(scores, axis=-1, keepdims=True)
    raised = jnp.exp(scores - top)
    return (raised / jnp.sum(raised, axis=-1, keepdims=True)).astype(jnp.bfloat16)


def row_attend(queries, keys, values, head_count):
    depth = queries.shape[0]
    query_len = queries.shape[1]
    key_len = keys.shape[1]
    head_size = queries.shape[2] // head_count
    query_cols = jnp.arange(query_len, dtype=jnp.int32)
    key_cols = jnp.arange(key_len, dtype=jnp.int32)
    visible = query_cols[:, None] >= key_cols[None, :]

    def split_heads(block, length):
        return jnp.moveaxis(block.reshape(depth, length, head_count, head_size), 2, 0)

    def one_head(parts):
        head_q, head_k, head_v = parts
        scores = jnp.einsum(
            "rqd,rkd->rqk", head_q, head_k, preferred_element_type=jnp.float32
        ) * head_size ** (-0.5)
        soft_weights = softmax_round(scores, visible)
        return jnp.einsum(
            "rqk,rkd->rqd", soft_weights, head_v, preferred_element_type=jnp.float32
        ).astype(jnp.bfloat16)

    mixed = lax.map(
        one_head,
        (split_heads(queries, query_len), split_heads(keys, key_len), split_heads(values, key_len)),
    )
    return jnp.moveaxis(mixed, 0, 2).reshape(depth, query_len, head_count * head_size)


def col_attend(queries, key_value, query_rows, query_starts):
    row_len, column_count, feature_width = queries.shape
    key_len = key_value.shape[0]
    head_size = key_value.shape[2] // 2
    head_count = feature_width // head_size
    split = queries.reshape(row_len, column_count, head_count, head_size)
    keys = key_value[..., :head_size]
    values = key_value[..., head_size:]
    scores = jnp.einsum(
        "qchd,kcd->chqk", split, keys, preferred_element_type=jnp.float32
    ) * head_size ** (-0.5)
    key_rows = jnp.arange(key_len, dtype=jnp.int32)
    visible = (key_rows[None, :] <= query_rows[:, None]) & (
        key_rows[None, :] >= query_starts[:, None]
    )
    soft_weights = softmax_round(scores, visible)
    mixed = jnp.einsum(
        "chqk,kcd->qchd", soft_weights, values, preferred_element_type=jnp.float32
    ).astype(jnp.bfloat16)
    return mixed.reshape(row_len, column_count, feature_width)


def upsample(grid):
    return jnp.repeat(jnp.repeat(grid, 2, axis=0), 2, axis=1)


def conv_three(padded, kernel):
    height = padded.shape[0] - 2
    breadth = padded.shape[1] - 2
    total = jnp.zeros((height, breadth, kernel.shape[3]), jnp.float32)
    for shift_down in range(3):
        for shift_right in range(3):
            window = padded[shift_down : shift_down + height, shift_right : shift_right + breadth]
            total = total + matmul(window, kernel[shift_down, shift_right])
    return total


def per_device(
    codes,
    starts,
    embed,
    gain_one,
    row_qkv,
    row_out,
    gain_two,
    col_qkv,
    col_out,
    gain_three,
    mlp_in,
    mlp_out,
    project,
    conv_one,
    conv_two,
):
    row_count, column_count = codes.shape
    model_width = embed.shape[1]
    vocab_ids = jnp.arange(embed.shape[0], dtype=jnp.int32)
    one_hot = (codes[..., None] == vocab_ids).astype(jnp.bfloat16)
    hidden = matmul(one_hot, embed)
    normed = norm_round(hidden, gain_one)
    projected = matmul(normed, row_qkv).astype(jnp.bfloat16)
    queries = projected[..., :model_width]
    keys = projected[..., model_width : 2 * model_width]
    values = projected[..., 2 * model_width :]
    local_heads = HEADS // lax.axis_size("col")
    parts = (
        lax.all_to_all(queries, "col", split_axis=2, concat_axis=1, tiled=True),
        lax.all_to_all(keys, "col", split_axis=2, concat_axis=1, tiled=True),
        lax.all_to_all(values, "col", split_axis=2, concat_axis=1, tiled=True),
    )
    mixed = row_attend(parts[0], parts[1], parts[2], local_heads)
    row_mixed = lax.all_to_all(mixed, "col", split_axis=1, concat_axis=2, tiled=True)
    hidden = hidden + matmul(row_mixed, row_out)
    normed = norm_round(hidden, gain_two)
    projected = matmul(normed, col_qkv).astype(jnp.bfloat16)
    col_queries = projected[..., :model_width]
    key_value = projected[..., model_width:]
    slots = lax.axis_size("row")
    per_slot = column_count // slots
    slotted_q = col_queries.reshape(row_count, slots, per_slot, model_width)
    slotted_kv = key_value.reshape(row_count, slots, per_slot, key_value.shape[2])
    parts = (
        lax.all_to_all(slotted_q, "row", split_axis=1, concat_axis=0, tiled=True),
        lax.all_to_all(slotted_kv, "row", split_axis=1, concat_axis=0, tiled=True),
    )
    total_rows = parts[0].shape[0]
    taken = parts[0].shape[2]
    flat_q = parts[0].reshape(total_rows, taken, parts[0].shape[3])
    flat_kv = parts[1].reshape(total_rows, taken, parts[1].shape[3])
    mixed = col_attend(flat_q, flat_kv, jnp.arange(total_rows, dtype=jnp.int32), starts)
    spread = mixed.reshape(total_rows, 1, taken, mixed.shape[2])
    returned = lax.all_to_all(spread, "row", split_axis=0, concat_axis=1, tiled=True)
    col_mixed = returned.reshape(row_count, column_count, model_width)
    hidden = hidden + matmul(col_mixed, col_out)
    normed = norm_round(hidden, gain_three)
    inner = jax.nn.silu(matmul(normed, mlp_in)).astype(jnp.bfloat16)
    block_out = hidden + matmul(inner, mlp_out)
    coarse = matmul(block_out.astype(jnp.bfloat16), project).astype(jnp.bfloat16)
    upsampled = upsample(coarse)
    extended = padded_2(coarse, (("row", 0), ("col", 1)), 1)
    widened = upsample(extended)
    first_raw = jax.nn.silu(conv_three(widened, conv_one))
    fine_rows = (
        2 * row_count * lax.axis_index("row") - 1 + jnp.arange(2 * row_count + 2, dtype=jnp.int32)
    )
    fine_cols = (
        2 * column_count * lax.axis_index("col")
        - 1
        + jnp.arange(2 * column_count + 2, dtype=jnp.int32)
    )
    rows_inside = (fine_rows >= 0) & (fine_rows < 2 * row_count * lax.axis_size("row"))
    cols_inside = (fine_cols >= 0) & (fine_cols < 2 * column_count * lax.axis_size("col"))
    inside = rows_inside[:, None] & cols_inside[None, :]
    first = jnp.where(inside[..., None], first_raw, 0.0).astype(jnp.bfloat16)
    second = conv_three(first, conv_two)
    image = upsampled.astype(jnp.float32) + second
    return (block_out, image)


def solution(mesh):
    in_specs = (
        P("row", "col"),
        P(),
        P(),
        P(),
        P(),
        P(),
        P(),
        P(),
        P(),
        P(),
        P(),
        P(),
        P(),
        P(),
        P(),
    )
    out_specs = (P("row", "col", None), P("row", "col", None))
    return jax.shard_map(
        per_device, mesh=mesh, in_specs=in_specs, out_specs=out_specs, check_vma=False
    )
```

profile of v0, /device:TPU:29, one launch (start us, length us, event | category | flops | bytes accessed | tf_op | source)
XLA Modules:
  0.0 547.8 jit_solution(2994674358862829613)
XLA Ops:
  3.3 3.8 convolution_convert_fusion
  9.8 6.6 %copy.39 = bf16[32,64,512]{1,0,2:T(8,128)(2,1)} copy(bf16[32,64,512]{2,1,0:T(8,128)(2,1)S(1)} %get-tuple-element.16) | data formatting | bytes 4194304 | tf_op jit(solution)/shard_map/slice | solution.py:132
  16.4 7.6 %reshape.146 = bf16[8,2,65536]{2,1,0:T(2,128)(2,1)} reshape(bf16[512,32,64]{2,1,0:T(8,128)(2,1)} %bitcast.215) | data formatting | bytes 4194304
  24.0 4.8 all-to-all-start
  28.8 7.4 %copy.41 = bf16[32,64,512]{1,0,2:T(8,128)(2,1)} copy(bf16[32,64,512]{2,1,0:T(8,128)(2,1)} %get-tuple-element.14) | data formatting | bytes 4194304 | tf_op jit(solution)/shard_map/slice | solution.py:133
  36.2 7.5 %reshape.148 = bf16[8,2,65536]{2,1,0:T(2,128)(2,1)} reshape(bf16[512,32,64]{2,1,0:T(8,128)(2,1)} %bitcast.216) | data formatting | bytes 4194304
  43.7 9.2 %all-to-all-done = bf16[8,2,65536]{2,1,0:T(2,128)(2,1)S(1)} async-done(((bf16[8,2,65536]{2,1,0:T(2,128)(2,1)}), bf16[8,2,65536]{2,1,0:T(2,128)(2,1)S(1)}, u32[]{:S(2)}, u32[]{:S(2)}) %all-to-all-start) | async-done | bytes 2097184 | tf_op jit(solution)/shard_map/all_to_all | solution.py:137
  52.9 6.3 %all-to-all-start.1 = ((bf16[8,2,65536]{2,1,0:T(2,128)(2,1)}), bf16[8,2,65536]{2,1,0:T(2,128)(2,1)}, u32[]{:S(2)}, u32[]{:S(2)}) async-start(bf16[8,2,65536]{2,1,0:T(2,128)(2,1)} %reshape.148), calls=%async_computation.1 | async-start | bytes 4194304 | tf_op jit(solution)/shard_map/all_to_all | solution.py:138
  59.2 7.4 %copy.43 = bf16[32,64,512]{1,0,2:T(8,128)(2,1)} copy(bf16[32,64,512]{2,1,0:T(8,128)(2,1)} %get-tuple-element.15) | data formatting | bytes 4194304 | tf_op jit(solution)/shard_map/slice | solution.py:134
  66.6 7.6 %reshape.144 = bf16[8,2,65536]{2,1,0:T(2,128)(2,1)} reshape(bf16[512,32,64]{2,1,0:T(8,128)(2,1)} %bitcast.217) | data formatting | bytes 4194304
  74.1 9.4 %all-to-all-done.1 = bf16[8,2,65536]{2,1,0:T(2,128)(2,1)} async-done(((bf16[8,2,65536]{2,1,0:T(2,128)(2,1)}), bf16[8,2,65536]{2,1,0:T(2,128)(2,1)}, u32[]{:S(2)}, u32[]{:S(2)}) %all-to-all-start.1) | async-done | bytes 2097184 | tf_op jit(solution)/shard_map/all_to_all | solution.py:138
  83.5 6.7 %all-to-all-start.2 = ((bf16[8,2,65536]{2,1,0:T(2,128)(2,1)}), bf16[8,2,65536]{2,1,0:T(2,128)(2,1)}, u32[]{:S(2)}, u32[]{:S(2)}) async-start(bf16[8,2,65536]{2,1,0:T(2,128)(2,1)} %reshape.144), calls=%async_computation.2 | async-start | bytes 4194304 | tf_op jit(solution)/shard_map/all_to_all | solution.py:139
  90.3 5.0 reshape.147
  95.2 6.8 %copy.75 = bf16[32,64,8,64]{1,2,3,0:T(8,128)(2,1)} copy(bf16[32,64,8,64]{1,0,3,2:T(8,128)(2,1)} %bitcast.219) | data formatting | bytes 4194304 | tf_op jit(solution)/shard_map/all_to_all | solution.py:137
  102.1 5.4 squeeze.67
  107.5 7.4 %reshape.149 = bf16[512,32,64]{2,1,0:T(8,128)(2,1)} reshape(bf16[8,2,65536]{2,1,0:T(2,128)(2,1)} %all-to-all-done.1) | data formatting | bytes 4194304
  114.9 6.8 %copy.74 = bf16[32,64,8,64]{1,2,3,0:T(8,128)(2,1)} copy(bf16[32,64,8,64]{1,0,3,2:T(8,128)(2,1)} %bitcast.221) | data formatting | bytes 4194304 | tf_op jit(solution)/shard_map/all_to_all | solution.py:138
  121.7 6.5 %squeeze.68 = bf16[32,512,64]{1,2,0:T(8,128)(2,1)} reshape(bf16[32,8,64,64]{2,1,3,0:T(8,128)(2,1)} %bitcast.222) | data formatting | bytes 4194304 | tf_op jit(solution)/shard_map/while/body/jit(dynamic_index_in_dim)/squeeze | solution.py:64
  128.2 7.4 %reshape.145 = bf16[512,32,64]{2,1,0:T(8,128)(2,1)} reshape(bf16[8,2,65536]{2,1,0:T(2,128)(2,1)} %all-to-all-done.2) | data formatting | bytes 4194304
  135.5 6.8 %copy.73 = bf16[32,64,8,64]{1,2,3,0:T(8,128)(2,1)} copy(bf16[32,64,8,64]{1,0,3,2:T(8,128)(2,1)} %bitcast.223) | data formatting | bytes 4194304 | tf_op jit(solution)/shard_map/all_to_all | solution.py:139
  142.4 6.6 %squeeze.69 = bf16[32,512,64]{1,2,0:T(8,128)(2,1)} reshape(bf16[32,8,64,64]{2,1,3,0:T(8,128)(2,1)} %bitcast.224) | data formatting | bytes 4194304 | tf_op jit(solution)/shard_map/while/body/jit(dynamic_index_in_dim)/squeeze | solution.py:64
  149.0 19.2 %fusion.129 = (f32[32,512]{1,0:T(8,128)S(1)}, f32[32,512,512]{1,2,0:T(8,128)}) fusion(pred[512,512]{0,1:T(8,128)(4,1)S(1)} %iota_compare_fusion.4, bf16[32,512,64]{1,2,0:T(8,128)(2,1)S(1)} %squeeze.67, bf16[32,512,64]{1,2,0:T(8,128)(2,1)} %squeeze.68), kind=kOutput, calls=%fused_computation.158 | convolution fusion | flops 1107296768 | bytes 38076416 | tf_op jit(solution)/shard_map/while/body/eval_jaxpr/sub | solution.py:38
  168.2 12.8 %fusion.70 = bf16[32,512,64]{1,2,0:T(8,128)(2,1)S(1)} fusion(bf16[32,512,64]{1,2,0:T(8,128)(2,1)} %squeeze.69, f32[32,512,512]{1,2,0:T(8,128)} %get-tuple-element.30, f32[32,512]{1,0:T(8,128)S(1)} %get-tuple-element.29), kind=kOutput, calls=%fused_computation.88 | convolution fusion | flops 1091567616 | bytes 37814272 | tf_op jit(solution)/shard_map/while/body/eval_jaxpr/rqk,rkd->rqd/dot_general | solution.py:60
  181.0 6.6 %copy.46 = bf16[32,512,64]{2,0,1:T(8,128)(2,1)} copy(bf16[32,512,64]{1,2,0:T(8,128)(2,1)S(1)} %fusion.70) | data formatting | bytes 4194304 | tf_op jit(solution)/shard_map/while/body/eval_jaxpr/convert_element_type | solution.py:62
  187.6 6.4 %reshape.150 = bf16[8,2,65536]{2,1,0:T(2,128)(2,1)S(1)} reshape(bf16[512,32,64]{2,1,0:T(8,128)(2,1)} %bitcast.218) | data formatting | bytes 4194304
  194.0 28.5 %all_to_all.108 = bf16[8,2,65536]{2,1,0:T(2,128)(2,1)} all-to-all(bf16[8,2,65536]{2,1,0:T(2,128)(2,1)S(1)} %reshape.150), channel_id=1, replica_groups=mesh['row'=16,'col'=8] {'col'}, dimensions={0} | all-to-all | bytes 4194304 | tf_op jit(solution)/shard_map/all_to_all | solution.py:142
  222.4 7.4 %reshape.151 = bf16[512,32,64]{2,1,0:T(8,128)(2,1)} reshape(bf16[8,2,65536]{2,1,0:T(2,128)(2,1)} %all_to_all.108) | data formatting | bytes 4194304
  229.8 6.8 %copy.72 = bf16[32,8,64,64]{3,1,2,0:T(8,128)(2,1)} copy(bf16[32,8,64,64]{3,0,2,1:T(8,128)(2,1)} %bitcast.225) | data formatting | bytes 4194304 | tf_op jit(solution)/shard_map/all_to_all | solution.py:142
  236.7 5.4 all_to_all.91
  242.2 3.6 multiply_reduce_fusion.1
  250.9 10.4 %all-to-all-start.4 = ((bf16[32,16,4,128]{3,0,2,1:T(8,128)(2,1)}), bf16[32,16,4,128]{3,0,2,1:T(8,128)(2,1)S(1)}, u32[]{:S(2)}, u32[]{:S(2)}) async-start(bf16[32,16,4,128]{3,0,2,1:T(8,128)(2,1)} %copy.48), calls=%async_computation.4 | async-start | bytes 1048576 | tf_op jit(solution)/shard_map/all_to_all | solution.py:154
  264.0 7.0 %all-to-all-done.4 = bf16[32,16,4,128]{3,0,2,1:T(8,128)(2,1)S(1)} async-done(((bf16[32,16,4,128]{3,0,2,1:T(8,128)(2,1)}), bf16[32,16,4,128]{3,0,2,1:T(8,128)(2,1)S(1)}, u32[]{:S(2)}, u32[]{:S(2)}) %all-to-all-start.4) | async-done | bytes 524320 | tf_op jit(solution)/shard_map/all_to_all | solution.py:154
  271.0 6.8 %all-to-all-start.5 = ((bf16[32,16,4,512]{3,0,2,1:T(8,128)(2,1)}), bf16[32,16,4,512]{3,0,2,1:T(8,128)(2,1)S(1)}, u32[]{:S(2)}, u32[]{:S(2)}) async-start(bf16[32,16,4,512]{3,0,2,1:T(8,128)(2,1)} %bitcast.22), calls=%async_computation.5 | async-start | bytes 4194304 | tf_op jit(solution)/shard_map/all_to_all | solution.py:153
  278.0 26.3 %all-to-all-done.5 = bf16[32,16,4,512]{3,0,2,1:T(8,128)(2,1)S(1)} async-done(((bf16[32,16,4,512]{3,0,2,1:T(8,128)(2,1)}), bf16[32,16,4,512]{3,0,2,1:T(8,128)(2,1)S(1)}, u32[]{:S(2)}, u32[]{:S(2)}) %all-to-all-start.5) | async-done | bytes 2097184 | tf_op jit(solution)/shard_map/all_to_all | solution.py:153
  311.0 17.8 %fusion.12 = f32[4,512,512,8]{2,1,3,0:T(8,128)} fusion(bf16[512,4,8,64]{3,2,0,1:T(8,128)(2,1)} %reshape_reshape.6, bf16[512,4,128]{2,0,1:T(8,128)(2,1)S(1)} %bitcast.231), kind=kOutput, calls=%fused_computation.21 | convolution fusion | flops 1073741824 | bytes 36175872 | tf_op jit(solution)/shard_map/qchd,kcd->chqk/dot_general | solution.py:79
  328.7 34.3 %fusion.130 = (f32[4,8,512]{2,1,0:T(8,128)S(1)}, f32[4,8,512,512]{2,3,1,0:T(8,128)}) fusion(f32[4,512,512,8]{2,1,3,0:T(8,128)} %fusion.12, pred[512,512]{0,1:T(8,128)(4,1)S(1)} %fusion.80), kind=kOutput, calls=%fused_computation.159 | output fusion | flops 50332160 | bytes 67436544 | tf_op jit(solution)/shard_map/sub | solution.py:38
  363.1 12.9 %fusion.69 = bf16[4,64,8,512]{3,1,2,0:T(8,128)(2,1)S(1)} fusion(f32[4,8,512,512]{2,3,1,0:T(8,128)} %get-tuple-element.34, f32[4,8,512]{2,1,0:T(8,128)S(1)} %get-tuple-element.33, bf16[512,4,128]{2,0,1:T(8,128)(2,1)S(1)} %bitcast.232), kind=kOutput, calls=%fused_computation.87 | convolution fusion | flops 1091567616 | bytes 36241408 | tf_op jit(solution)/shard_map/chqk,kcd->qchd/dot_general | solution.py:87
  379.0 6.6 %all-to-all-start.6 = ((bf16[512,1,4,512]{3,2,1,0:T(4,128)(2,1)}), bf16[512,1,4,512]{3,2,1,0:T(4,128)(2,1)S(1)}, u32[]{:S(2)}, u32[]{:S(2)}) async-start(bf16[512,1,4,512]{3,2,1,0:T(4,128)(2,1)} %copy.56), calls=%async_computation.6 | async-start | bytes 4194304 | tf_op jit(solution)/shard_map/all_to_all | solution.py:162
  385.6 26.5 %all-to-all-done.6 = bf16[512,1,4,512]{3,2,1,0:T(4,128)(2,1)S(1)} async-done(((bf16[512,1,4,512]{3,2,1,0:T(4,128)(2,1)}), bf16[512,1,4,512]{3,2,1,0:T(4,128)(2,1)S(1)}, u32[]{:S(2)}, u32[]{:S(2)}) %all-to-all-start.6) | async-done | bytes 2097184 | tf_op jit(solution)/shard_map/all_to_all | solution.py:162
  416.2 6.2 %multiply_reduce_fusion = (f32[32,64]{1,0:T(8,128)S(1)}, f32[32,64,512]{2,1,0:T(8,128)}) fusion(f32[32,64,512]{2,1,0:T(8,128)} %copy-done.2, bf16[32,64,512]{2,1,0:T(8,128)(2,1)} %reshape.113, bf16[512,512]{1,0:T(8,128)(2,1)S(1)} %copy-done.7), kind=kOutput, calls=%fused_computation.29 | convolution fusion | flops 1076885504 | bytes 11018240 | tf_op jit(solution)/shard_map/...i,ij->...j/dot_general | solution.py:32
  422.5 8.9 %fusion.37 = f32[32,64,512]{2,1,0:T(8,128)} fusion(f32[32,64,512]{2,1,0:T(8,128)} %get-tuple-element.36, f32[512]{0:T(512)S(1)} %copy-done.15, f32[32,64]{1,0:T(8,128)S(1)} %add_rsqrt_fusion, bf16[1024,512]{1,0:T(8,128)(2,1)S(1)} %copy-done.13, bf16[512,1024]{1,0:T(8,128)(2,1)} %param.25), kind=kOutput, calls=%fused_computation.59 | convolution fusion | flops 4309647360 | bytes 10496000 | tf_op jit(solution)/shard_map/...i,ij->...j/dot_general | solution.py:32
  434.3 3.7 collective-permute-start
  439.9 5.5 %collective-permute-done.1 = bf16[1,64,128]{2,1,0:T(8,128)(2,1)S(1)} collective-permute-done((bf16[1,64,128]{2,1,0:T(8,128)(2,1)S(1)}, bf16[1,64,128]{2,1,0:T(8,128)(2,1)S(1)}, u32[]{:S(2)}, u32[]{:S(2)}) %collective-permute-start.1) | collective-permute-done | bytes 16416 | tf_op jit(solution)/shard_map/ppermute | solution.py:21
  445.5 5.7 %collective-permute-start.2 = (bf16[34,1,128]{2,1,0:T(2,128)(2,1)S(1)}, bf16[34,1,128]{2,1,0:T(2,128)(2,1)S(1)}, u32[]{:S(2)}, u32[]{:S(2)}) collective-permute-start(bf16[34,1,128]{2,1,0:T(2,128)(2,1)S(1)} %get-tuple-element.17), channel_id=1, source_target_pairs={{0,1},{1,2},{2,3},{3,4},{4,5},{5,6},{6,7},{8,9},{9,10},{10,11},{11... | collective-permute-start | bytes 26120 | tf_op jit(solution)/shard_map/ppermute | solution.py:18
  453.2 4.6 collective-permute-done.3
  461.0 5.1 reshape.115
  493.9 13.2 %select_convert_fusion = bf16[66,130,128]{2,1,0:T(8,128)(2,1)S(1)} fusion(f32[66,130,128]{2,1,0:T(8,128)} %fusion.18, f32[66,130,128]{2,1,0:T(8,128)} %fusion.20, f32[66,130,128]{2,1,0:T(8,128)} %fusion.22, f32[66,130,128]{2,1,0:T(8,128)} %fusion.24, f32[66,130,128]{2,1,0:T(8,128)} %fusion.26, f32[66,130,128]{2,1,0:T(8,128)} %fusion.28, ...), kind=kOutput, calls=%fused_computation.20 | convolution fusion | flops 296524800 | bytes 39689216 | tf_op jit(solution)/shard_map/...i,ij->...j/dot_general | solution.py:32
  532.2 15.0 %add_add_fusion = f32[64,128,128]{2,1,0:T(8,128)} fusion(f32[64,128,128]{2,1,0:T(8,128)} %bitcast.214, f32[64,128,128]{2,1,0:T(8,128)} %fusion.39, f32[64,128,128]{2,1,0:T(8,128)} %fusion.41, f32[64,128,128]{2,1,0:T(8,128)} %fusion.43, f32[64,128,128]{2,1,0:T(8,128)} %fusion.45, f32[64,128,128]{2,1,0:T(8,128)} %fusion.47, f32[64,128,128]{2,1,0:T(8,128)} %fusion.49, ...), kind=kOutput, calls=%fused_computation.27 | convolution fusion | flops 277872640 | bytes 44072960 | tf_op jit(solution)/shard_map/...i,ij->...j/dot_general | solution.py:32
  (83 shorter events, 90.2 us)
Async XLA Ops:
  0.6 2.7 copy-start
  0.6 2.7 copy-start.14
  3.3 3.8 copy-start.4
  24.0 28.9 %all-to-all-start = ((bf16[8,2,65536]{2,1,0:T(2,128)(2,1)}), bf16[8,2,65536]{2,1,0:T(2,128)(2,1)S(1)}, u32[]{:S(2)}, u32[]{:S(2)}) async-start(bf16[8,2,65536]{2,1,0:T(2,128)(2,1)} %reshape.146), calls=%async_computation | async-start | bytes 4194304 | tf_op jit(solution)/shard_map/all_to_all | solution.py:137
  52.9 30.6 %all-to-all-start.1 = ((bf16[8,2,65536]{2,1,0:T(2,128)(2,1)}), bf16[8,2,65536]{2,1,0:T(2,128)(2,1)}, u32[]{:S(2)}, u32[]{:S(2)}) async-start(bf16[8,2,65536]{2,1,0:T(2,128)(2,1)} %reshape.148), calls=%async_computation.1 | async-start | bytes 4194304 | tf_op jit(solution)/shard_map/all_to_all | solution.py:138
  83.5 44.6 %all-to-all-start.2 = ((bf16[8,2,65536]{2,1,0:T(2,128)(2,1)}), bf16[8,2,65536]{2,1,0:T(2,128)(2,1)}, u32[]{:S(2)}, u32[]{:S(2)}) async-start(bf16[8,2,65536]{2,1,0:T(2,128)(2,1)} %reshape.144), calls=%async_computation.2 | async-start | bytes 4194304 | tf_op jit(solution)/shard_map/all_to_all | solution.py:139
  236.7 5.5 copy-start.6
  242.1 5.7 %copy-start.5 = (bf16[512,640]{1,0:T(8,128)(2,1)S(1)}, bf16[512,640]{1,0:T(8,128)(2,1)}, u32[]{:S(2)}) copy-start(bf16[512,640]{1,0:T(8,128)(2,1)} %param.22) | copy-start | bytes 1966084
  242.1 5.6 %copy-start.12 = (f32[512]{0:T(512)S(1)}, f32[512]{0:T(512)}, u32[]{:S(2)}) copy-start(f32[512]{0:T(512)} %param.21) | copy-start | bytes 6148
  245.8 2.0 copy-start.2
  250.9 20.1 %all-to-all-start.4 = ((bf16[32,16,4,128]{3,0,2,1:T(8,128)(2,1)}), bf16[32,16,4,128]{3,0,2,1:T(8,128)(2,1)S(1)}, u32[]{:S(2)}, u32[]{:S(2)}) async-start(bf16[32,16,4,128]{3,0,2,1:T(8,128)(2,1)} %copy.48), calls=%async_computation.4 | async-start | bytes 1048576 | tf_op jit(solution)/shard_map/all_to_all | solution.py:154
  261.5 16.3 %copy-start.11 = (s32[512]{0:T(512)S(1)}, s32[512]{0:T(512)}, u32[]{:S(2)}) copy-start(s32[512]{0:T(512)} %param.16) | copy-start | bytes 6148
  271.0 33.3 %all-to-all-start.5 = ((bf16[32,16,4,512]{3,0,2,1:T(8,128)(2,1)}), bf16[32,16,4,512]{3,0,2,1:T(8,128)(2,1)S(1)}, u32[]{:S(2)}, u32[]{:S(2)}) async-start(bf16[32,16,4,512]{3,0,2,1:T(8,128)(2,1)} %bitcast.22), calls=%async_computation.5 | async-start | bytes 4194304 | tf_op jit(solution)/shard_map/all_to_all | solution.py:153
  304.3 1.3 copy-start.3
  379.0 33.1 %all-to-all-start.6 = ((bf16[512,1,4,512]{3,2,1,0:T(4,128)(2,1)}), bf16[512,1,4,512]{3,2,1,0:T(4,128)(2,1)S(1)}, u32[]{:S(2)}, u32[]{:S(2)}) async-start(bf16[512,1,4,512]{3,2,1,0:T(4,128)(2,1)} %copy.56), calls=%async_computation.6 | async-start | bytes 4194304 | tf_op jit(solution)/shard_map/all_to_all | solution.py:162
  412.6 3.7 copy-start.7
  416.2 6.2 %copy-start.13 = (bf16[1024,512]{1,0:T(8,128)(2,1)S(1)}, bf16[1024,512]{1,0:T(8,128)(2,1)}, u32[]{:S(2)}) copy-start(bf16[1024,512]{1,0:T(8,128)(2,1)} %param.26) | copy-start | bytes 3145732
  416.2 6.2 %copy-start.15 = (f32[512]{0:T(512)S(1)}, f32[512]{0:T(512)}, u32[]{:S(2)}) copy-start(f32[512]{0:T(512)} %param.24) | copy-start | bytes 6148
  422.5 8.9 %copy-start.10 = (bf16[512,128]{1,0:T(8,128)(2,1)S(1)}, bf16[512,128]{1,0:T(8,128)(2,1)}, u32[]{:S(2)}) copy-start(bf16[512,128]{1,0:T(8,128)(2,1)} %param.27) | copy-start | bytes 393220
  434.3 5.7 %collective-permute-start = (bf16[1,64,128]{2,1,0:T(8,128)(2,1)S(1)}, bf16[1,64,128]{2,1,0:T(8,128)(2,1)S(1)}, u32[]{:S(2)}, u32[]{:S(2)}) collective-permute-start(bf16[1,64,128]{2,1,0:T(8,128)(2,1)S(1)} %get-tuple-element.25), channel_id=1, source_target_pairs={{0,8},{8,16},{16,24},{24,32},{32,40},{40,48},{48,56},{56,64},{64,7... | collective-permute-start | bytes 49160 | tf_op jit(solution)/shard_map/ppermute | solution.py:18
  438.0 7.5 %collective-permute-start.1 = (bf16[1,64,128]{2,1,0:T(8,128)(2,1)S(1)}, bf16[1,64,128]{2,1,0:T(8,128)(2,1)S(1)}, u32[]{:S(2)}, u32[]{:S(2)}) collective-permute-start(bf16[1,64,128]{2,1,0:T(8,128)(2,1)S(1)} %get-tuple-element.26), channel_id=1, source_target_pairs={{8,0},{16,8},{24,16},{32,24},{40,32},{48,40},{56,48},{64,56},{72,6... | collective-permute-start | bytes 49160 | tf_op jit(solution)/shard_map/ppermute | solution.py:21
  445.5 7.7 %collective-permute-start.2 = (bf16[34,1,128]{2,1,0:T(2,128)(2,1)S(1)}, bf16[34,1,128]{2,1,0:T(2,128)(2,1)S(1)}, u32[]{:S(2)}, u32[]{:S(2)}) collective-permute-start(bf16[34,1,128]{2,1,0:T(2,128)(2,1)S(1)} %get-tuple-element.17), channel_id=1, source_target_pairs={{0,1},{1,2},{2,3},{3,4},{4,5},{5,6},{6,7},{8,9},{9,10},{10,11},{11... | collective-permute-start | bytes 26120 | tf_op jit(solution)/shard_map/ppermute | solution.py:18
  451.1 6.6 %collective-permute-start.3 = (bf16[34,1,128]{2,1,0:T(2,128)(2,1)S(1)}, bf16[34,1,128]{2,1,0:T(2,128)(2,1)S(1)}, u32[]{:S(2)}, u32[]{:S(2)}) collective-permute-start(bf16[34,1,128]{2,1,0:T(2,128)(2,1)S(1)} %get-tuple-element.24), channel_id=1, source_target_pairs={{1,0},{2,1},{3,2},{4,3},{5,4},{6,5},{7,6},{9,8},{10,9},{11,10},{12... | collective-permute-start | bytes 26120 | tf_op jit(solution)/shard_map/ppermute | solution.py:21
  458.2 7.8 %copy-start.8 = (bf16[3,3,128,128]{3,2,1,0:T(8,128)(2,1)S(1)}, bf16[3,3,128,128]{3,2,1,0:T(8,128)(2,1)}, u32[]{:S(2)}) copy-start(bf16[3,3,128,128]{3,2,1,0:T(8,128)(2,1)} %param.28) | copy-start | bytes 884740
  493.9 13.2 %copy-start.9 = (bf16[3,3,128,128]{3,2,1,0:T(8,128)(2,1)S(1)}, bf16[3,3,128,128]{3,2,1,0:T(8,128)(2,1)}, u32[]{:S(2)}) copy-start(bf16[3,3,128,128]{3,2,1,0:T(8,128)(2,1)} %param.29) | copy-start | bytes 884740
  532.2 15.1 %copy-start.1 = (bf16[512,1536]{1,0:T(8,128)(2,1)S(1)}, bf16[512,1536]{1,0:T(8,128)(2,1)}, u32[]{:S(2)}) copy-start(bf16[512,1536]{1,0:T(8,128)(2,1)} %param.19) | copy-start | bytes 4718596
where the time goes:
time: 557 us; the launch traced here: 548 us
  local copies, waits for them, and re-layouts  170 us (31%)
  matrix products  170 us (31%)
  waiting for transfers between devices  88.5 us (16%)
  starting transfers between devices  54.7 us (10%)
  other arithmetic  35 us (6%)
  blocking collectives  28.5 us (5%)
    dot_general x25, matrix products, matmul(): jnp.einsum('...i,ij->...j', left, right, preferred_element_type=jnp.float32)  107 us
    unnamed x40, local copies, waits for them, and re-layouts  59.6 us
    sub x1, other arithmetic, softmax_round(): raised = jnp.exp(scores - top)  34.3 us
    all_to_all x1, blocking collectives, per_device(): lax.all_to_all(mixed, 'col', split_axis=1, concat_axis=2, tiled=True)  28.5 us
    all_to_all x1, waiting for transfers between devices, per_device(): lax.all_to_all(spread, 'row', split_axis=0, concat_axis=1, tiled=True)  26.5 us
    all_to_all x1, waiting for transfers between devices, per_device(): lax.all_to_all(slotted_q, 'row', split_axis=1, concat_axis=0, tiled=True)  26.3 us
    sub x1, matrix products, softmax_round(): raised = jnp.exp(scores - top)  19.2 us
    squeeze x3, local copies, waits for them, and re-layouts, row_attend(): lax.map(one_head, (split_heads(queries, query_len), split_heads(keys, key...  18.4 us
  transfers between devices with their start and end apart: 10, of which 7 were waited for; matrix products, arithmetic and copies ran while one was open for 13% of the time, Pallas kernels for 0%

commit v1 on v0

v1 whole, which is shorter than its diff:
```python
import math
import jax
import jax.numpy as jnp
from jax import lax
from jax.experimental import pallas as pl
from jax.experimental.pallas import tpu as pltpu
from jax.sharding import PartitionSpec as P

HEADS = 8
HD = 64
EPS = 1e-06
NEGATIVE = -1e30
LOG2E = math.log2(math.e)
F32 = jnp.float32
BF16 = jnp.bfloat16
VMEM_LIMIT = 56 * 1024 * 1024


def dot(left, right):
    return jnp.dot(left, right, preferred_element_type=F32)


def dot_t(left, right):
    return lax.dot_general(left, right, (((1,), (1,)), ((), ())), preferred_element_type=F32)


def norm_round(values, norm_gain):
    scale = lax.rsqrt(jnp.mean(values * values, axis=-1, keepdims=True) + EPS)
    return (values * scale * norm_gain).astype(BF16)


def silu(v):
    return v / (1.0 + jnp.exp(-v))


def lane_low(rows):
    return lax.broadcasted_iota(jnp.int32, (rows, 128), 1) < HD


def row_kernel(
    codes_ref, base_ref, embed_ref, g1_ref, wqkv_ref, wro_ref, g2_ref, wcol_ref,
    ar_ref, q2_ref, kv_ref,
    qtab, kz, vz, seen, tri, wq2,
):
    k = pl.program_id(0)
    vocab, width = embed_ref.shape
    rows = codes_ref.shape[0]
    tile = ar_ref.shape[0]
    per = tile // rows
    scale = (HD ** -0.5) * LOG2E

    @pl.when(k == 0)
    def _():
        normed = norm_round(embed_ref[...].astype(F32), g1_ref[...])
        low = lane_low(vocab)
        qtab[...] = (dot(normed, wqkv_ref[:, :width]) * scale).astype(BF16)
        keys = dot(normed, wqkv_ref[:, width : 2 * width])
        values = dot(normed, wqkv_ref[:, 2 * width :])
        for h in range(HEADS):
            p = h // 2
            mine = low if h % 2 == 0 else jnp.logical_not(low)
            sl = slice(p * 128, p * 128 + 128)
            kz[h] = jnp.where(mine, keys[:, sl], 0.0).astype(BF16)
            vz[h] = jnp.where(mine, values[:, sl], 1.0).astype(BF16)
        seen[...] = base_ref[...]
        out_t = lax.broadcasted_iota(jnp.int32, (tile, tile), 0)
        in_t = lax.broadcasted_iota(jnp.int32, (tile, tile), 1)
        tri[...] = jnp.where(
            (out_t % rows == in_t % rows) & (in_t // rows <= out_t // rows), 1.0, 0.0
        ).astype(BF16)
        lowd = lane_low(width)
        for p in range(HEADS // 2):
            w = wcol_ref[:, p * 128 : p * 128 + 128].astype(F32)
            wq2[:, (2 * p) * 128 : (2 * p + 1) * 128] = jnp.where(lowd, w, 0.0).astype(BF16)
            wq2[:, (2 * p + 1) * 128 : (2 * p + 2) * 128] = jnp.where(
                lowd, pltpu.roll(w, HD, 1), 0.0
            ).astype(BF16)

    rolled = pltpu.roll(codes_ref[...], 128 - per * k, 1)
    ids = lax.broadcasted_iota(jnp.int32, (rows, vocab), 1)
    one_hot = jnp.concatenate(
        [jnp.where(rolled[:, c : c + 1] == ids, 1.0, 0.0) for c in range(per)], axis=0
    ).astype(BF16)
    counts = dot(tri[...], one_hot) + jnp.concatenate([seen[...]] * per, axis=0)
    seen[...] = counts[tile - rows :]
    logn = jnp.where(counts > 0.5, jnp.log2(jnp.maximum(counts, 1.0)), NEGATIVE)
    emb = dot(one_hot, embed_ref[...])
    q = dot(one_hot, qtab[...]).astype(BF16)
    low = lane_low(tile)
    mixed = []
    for p in range(HEADS // 2):
        outs = []
        qp = q[:, p * 128 : p * 128 + 128]
        for h in (2 * p, 2 * p + 1):
            s = dot_t(qp, kz[h]) + logn
            top = jnp.max(s, axis=-1, keepdims=True)
            e = jnp.exp2(s - top).astype(BF16)
            outs.append(dot(e, vz[h]))
        num = jnp.where(low, outs[0], outs[1])
        den = pltpu.roll(jnp.where(low, outs[1], outs[0]), HD, 1)
        mixed.append((num / den).astype(BF16))
    after = emb + dot(jnp.concatenate(mixed, axis=1), wro_ref[...])
    ar_ref[...] = after
    normed = norm_round(after, g2_ref[...])
    q2 = dot(normed, wq2[...]) * scale
    lane = lax.broadcasted_iota(jnp.int32, (tile, 128), 1)
    row = lax.broadcasted_iota(jnp.int32, (tile, 128), 0) % rows
    mark = jnp.where(lane == HD + row, 1.0, 0.0)
    for h in range(HEADS):
        q2_ref[:, h * 128 : h * 128 + 128] = (q2[:, h * 128 : h * 128 + 128] + mark).astype(BF16)
    kv_ref[...] = dot(normed, wcol_ref[:, width:]).astype(BF16)


def full(shape):
    return pl.BlockSpec(shape, lambda *_: (0,) * len(shape))


def row_call(codes, base, embed, g1, wqkv, wro, g2, wcol, tokens):
    vocab, width = embed.shape
    rows = codes.shape[0]
    tile = rows * 8
    return pl.pallas_call(
        row_kernel,
        grid=(tokens // tile,),
        in_specs=[full(x.shape) for x in (codes, base, embed, g1, wqkv, wro, g2, wcol)],
        out_specs=[
            pl.BlockSpec((tile, width), lambda i: (i, 0)),
            pl.BlockSpec((tile, 2 * width), lambda i: (i, 0)),
            pl.BlockSpec((tile, 2 * HD), lambda i: (i, 0)),
        ],
        out_shape=[
            jax.ShapeDtypeStruct((tokens, width), F32),
            jax.ShapeDtypeStruct((tokens, 2 * width), BF16),
            jax.ShapeDtypeStruct((tokens, 2 * HD), BF16),
        ],
        scratch_shapes=[
            pltpu.VMEM((vocab, width), BF16),
            pltpu.VMEM((HEADS, vocab, 128), BF16),
            pltpu.VMEM((HEADS, vocab, 128), BF16),
            pltpu.VMEM((rows, vocab), F32),
            pltpu.VMEM((tile, tile), BF16),
            pltpu.VMEM((width, 2 * width), BF16),
        ],
        compiler_params=pltpu.CompilerParams(vmem_limit_bytes=VMEM_LIMIT),
        name="row_part",
    )(codes, base, embed, g1, wqkv, wro, g2, wcol)


def col_kernel(
    starts_ref, q2_ref, kv_ref, ar_ref, wco_ref, g3_ref, w1_ref, w2_ref, wp_ref,
    bo_ref, co_ref,
    bias, mixed,
):
    k = pl.program_id(0)
    rows = q2_ref.shape[1]
    per = q2_ref.shape[0]
    slots = kv_ref.shape[0]
    keys = slots * rows
    tile = per * rows

    @pl.when(k == 0)
    def _():
        first = lax.axis_index("row") * rows
        lane = lax.broadcasted_iota(jnp.int32, (keys, 128), 1)
        key_row = lax.broadcasted_iota(jnp.int32, (keys, 128), 0)
        query_row = first + lane - HD
        seen = (key_row <= query_row) & (key_row >= starts_ref[0:1, :])
        bias[...] = jnp.where((lane < HD) | seen, 0.0, NEGATIVE).astype(BF16)

    low_f = jnp.where(lane_low(keys), 1.0, 0.0)
    low_k = low_f.astype(BF16)
    high_k = (1.0 - low_f).astype(BF16)
    low = lane_low(rows)
    for c in range(per):
        kv = kv_ref[:, c].reshape(keys, 2 * HD)
        ka = kv * low_k + bias[...]
        va = kv * high_k + low_k
        q = q2_ref[c]
        q = jnp.concatenate([q[:, h * 128 : h * 128 + 128] for h in range(HEADS)], axis=0)
        s = dot_t(q, ka)
        top = jnp.max(s, axis=-1, keepdims=True)
        e = jnp.exp2(s - top).astype(BF16)
        o = dot(e, va)
        for p in range(HEADS // 2):
            even = o[(2 * p) * rows : (2 * p + 1) * rows]
            odd = o[(2 * p + 1) * rows : (2 * p + 2) * rows]
            keep = jnp.where(low, even, odd)
            other = pltpu.roll(jnp.where(low, odd, even), HD, 1)
            num = jnp.where(low, other, keep)
            den = jnp.where(low, keep, other)
            mixed[c * rows : (c + 1) * rows, p * 128 : p * 128 + 128] = (num / den).astype(BF16)
    after = ar_ref[...] + dot(mixed[...], wco_ref[...])
    normed = norm_round(after, g3_ref[...])
    inner = silu(dot(normed, w1_ref[...])).astype(BF16)
    out = after + dot(inner, w2_ref[...])
    coarse = dot(out.astype(BF16), wp_ref[...]).astype(BF16)
    bo_ref[...] = jnp.swapaxes(out.reshape(per, rows, out.shape[1]), 0, 1)
    co_ref[...] = coarse.reshape(per, rows, coarse.shape[1])


def col_call(starts, q2, kv, ar, wco, g3, w1, w2, wp):
    cols, rows, _ = q2.shape
    slots = kv.shape[0]
    width = ar.shape[1]
    channels = wp.shape[1]
    per = 8
    return pl.pallas_call(
        col_kernel,
        grid=(cols // per,),
        in_specs=[
            full(starts.shape),
            pl.BlockSpec((per, rows, 2 * width), lambda i: (i, 0, 0)),
            pl.BlockSpec((slots, per, rows, 2 * HD), lambda i: (0, i, 0, 0)),
            pl.BlockSpec((per * rows, width), lambda i: (i, 0)),
        ]
        + [full(x.shape) for x in (wco, g3, w1, w2, wp)],
        out_specs=[
            pl.BlockSpec((rows, per, width), lambda i: (0, i, 0)),
            pl.BlockSpec((per, rows, channels), lambda i: (i, 0, 0)),
        ],
        out_shape=[
            jax.ShapeDtypeStruct((rows, cols, width), F32),
            jax.ShapeDtypeStruct((cols, rows, channels), BF16),
        ],
        scratch_shapes=[
            pltpu.VMEM((slots * rows, 128), BF16),
            pltpu.VMEM((per * rows, width), BF16),
        ],
        compiler_params=pltpu.CompilerParams(vmem_limit_bytes=VMEM_LIMIT),
        name="col_part",
    )(starts, q2, kv, ar, wco, g3, w1, w2, wp)


def conv_kernel(ext_ref, k1_ref, k2_ref, out_ref, w1, w2, cat, fine):
    k = pl.program_id(0)
    erows, ring, ch = ext_ref.shape
    pairs = erows - 1
    cols = out_ref.shape[1] // 2
    step_rows = out_ref.shape[0]

    @pl.when(k == 0)
    def _():
        taps = [[k1_ref[y, x].astype(F32) for x in range(3)] for y in range(3)]
        none = jnp.zeros((ch, ch), F32)
        by_half = (
            ([taps[0][x] + taps[1][x] for x in range(3)], taps[2]),
            (taps[0], [taps[1][x] + taps[2][x] for x in range(3)]),
        )
        for half in range(2):
            for dy in range(2):
                t = by_half[half][dy]
                for b in range(2):
                    three = (t[0], t[1] + t[2], none) if b == 0 else (none, t[0] + t[1], t[2])
                    for dx in range(3):
                        w1[
                            (dy * 3 + dx) * ch : (dy * 3 + dx + 1) * ch,
                            (half * 2 + b) * ch : (half * 2 + b + 1) * ch,
                        ] = three[dx].astype(BF16)
        for dy in range(3):
            for s in range(4):
                for b in range(2):
                    w2[(dy * 4 + s) * ch : (dy * 4 + s + 1) * ch, b * ch : (b + 1) * ch] = (
                        k2_ref[dy, s - b] if 0 <= s - b <= 2 else none.astype(BF16)
                    )

        def widen(e, carry):
            x = ext_ref[e].astype(F32)
            cat[e] = jnp.concatenate(
                [pltpu.roll(x, 1, 0), x, pltpu.roll(x, ring - 1, 0)], axis=1
            ).astype(BF16)
            return carry

        lax.fori_loop(0, erows, widen, 0)
        place = lax.broadcasted_iota(jnp.int32, (ring, 128), 0)
        at_left = lax.axis_index("col") == 0
        at_right = lax.axis_index("col") == lax.axis_size("col") - 1
        col_keep = jnp.where(
            ((place == ring - 1) & at_left) | ((place == cols) & at_right), 0.0, 1.0
        )
        at_top = lax.axis_index("row") == 0
        at_bottom = lax.axis_index("row") == lax.axis_size("row") - 1
        group = 3

        def first_conv(g, carry):
            e0 = g * group
            left = jnp.concatenate(
                [
                    jnp.concatenate([cat[e0 + i], cat[e0 + i + 1]], axis=1)
                    for i in range(group)
                ],
                axis=0,
            )
            y = silu(dot(left, w1[...]))
            for i in range(group):
                for half in range(2):
                    f = 2 * (e0 + i) + half
                    outside = ((f == 0) & at_top) | ((f == 2 * pairs - 1) & at_bottom)
                    keep = jnp.where(outside, 0.0, 1.0) * col_keep
                    f0 = y[i * ring : (i + 1) * ring, (2 * half) * ch : (2 * half + 1) * ch] * keep
                    f1 = y[i * ring : (i + 1) * ring, (2 * half + 1) * ch : (2 * half + 2) * ch] * keep
                    fine[f] = jnp.concatenate(
                        [pltpu.roll(f1, 1, 0), f0, f1, pltpu.roll(f0, ring - 1, 0)], axis=1
                    ).astype(BF16)
            return carry

        lax.fori_loop(0, pairs // group, first_conv, 0)

    y0 = k * step_rows
    left = jnp.concatenate(
        [
            jnp.concatenate([fine[y0 + i + dy, 0:cols] for dy in range(3)], axis=1)
            for i in range(step_rows)
        ],
        axis=0,
    )
    second = dot(left, w2[...])
    for i in range(step_rows):
        up = ext_ref[k * (step_rows // 2) + i // 2 + 1, 0:cols].astype(F32)
        for b in range(2):
            out_ref[i, pl.ds(b, cols, stride=2), :] = (
                second[i * cols : (i + 1) * cols, b * ch : (b + 1) * ch] + up
            )


def conv_call(ext, k1, k2):
    erows, ring, ch = ext.shape
    fine_rows = 2 * (erows - 2)
    cols = ring - 16
    step_rows = 8
    return pl.pallas_call(
        conv_kernel,
        grid=(fine_rows // step_rows,),
        in_specs=[full(ext.shape), full(k1.shape), full(k2.shape)],
        out_specs=pl.BlockSpec((step_rows, 2 * cols, ch), lambda i: (i, 0, 0)),
        out_shape=jax.ShapeDtypeStruct((fine_rows, 2 * cols, ch), F32),
        scratch_shapes=[
            pltpu.VMEM((6 * ch, 4 * ch), BF16),
            pltpu.VMEM((12 * ch, 2 * ch), BF16),
            pltpu.VMEM((erows, ring, 3 * ch), BF16),
            pltpu.VMEM((fine_rows + 2, ring, 4 * ch), BF16),
        ],
        compiler_params=pltpu.CompilerParams(vmem_limit_bytes=VMEM_LIMIT),
        name="conv_part",
    )(ext, k1, k2)


def padded_2(block, sides, width):
    for axis, dim in sides:
        count = lax.axis_size(axis)
        forward = [(i, i + 1) for i in range(count - 1)]
        backward = [(target, source) for source, target in forward]
        low = lax.ppermute(
            lax.slice_in_dim(block, block.shape[dim] - width, None, axis=dim), axis, forward
        )
        high = lax.ppermute(lax.slice_in_dim(block, 0, width, axis=dim), axis, backward)
        block = jnp.concatenate([low, block, high], axis=dim)
    return block


def per_device(
    codes, starts, embed, gain_one, row_qkv, row_out, gain_two, col_qkv, col_out,
    gain_three, mlp_in, mlp_out, project, conv_one, conv_two,
):
    rows, cols = codes.shape
    vocab, width = embed.shape
    ids = jnp.arange(vocab, dtype=jnp.int32)
    mine = jnp.sum((codes[..., None] == ids).astype(F32), axis=1)
    every = lax.all_gather(mine, "col", axis=0)
    earlier = jnp.arange(every.shape[0]) < lax.axis_index("col")
    base = jnp.sum(jnp.where(earlier[:, None, None], every, 0.0), axis=0)
    wide = jnp.pad(codes, ((0, 0), (0, 128 - cols)))
    after_row, q2, kv = row_call(
        wide, base, embed, gain_one[None], row_qkv, row_out, gain_two[None], col_qkv, rows * cols
    )
    kv = kv.reshape(cols, rows, 2 * HD)
    kvs = lax.all_gather(kv, "row", axis=0)
    my_starts = lax.dynamic_slice_in_dim(starts, lax.axis_index("row") * rows, rows)
    my_starts = jnp.pad(my_starts, (HD, 128 - HD - rows))[None]
    block_out, coarse = col_call(
        my_starts, q2.reshape(cols, rows, 2 * width), kvs, after_row,
        col_out, gain_three[None], mlp_in, mlp_out, project,
    )
    coarse = jnp.swapaxes(coarse, 0, 1)
    ext = padded_2(coarse, (("row", 0), ("col", 1)), 1)
    ext = jnp.concatenate(
        [ext[:, 1:], jnp.zeros((rows + 2, 14, ext.shape[2]), BF16), ext[:, :1]], axis=1
    )
    image = conv_call(ext, conv_one, conv_two)
    return (block_out, image)


def solution(mesh):
    in_specs = (P("row", "col"),) + (P(),) * 14
    out_specs = (P("row", "col", None), P("row", "col", None))
    return jax.shard_map(
        per_device, mesh=mesh, in_specs=in_specs, out_specs=out_specs, check_vma=False
    )
```

time: 557 us -> 228 us (0.41)
  the two profiles are of different devices: /device:TPU:29 before, /device:TPU:3 now
where the time goes in v1:
time: 228 us; the launch traced here: 227 us
  waiting for transfers between devices  88.7 us (39%)
  Pallas kernels  82.2 us (36%)
  blocking collectives  23 us (10%)
  between operations  14.1 us (6%)
  starting transfers between devices  11.5 us (5%)
  local copies, waits for them, and re-layouts  4.06 us (2%)
  other arithmetic  3.2 us (1%)
    all_gather x1, waiting for transfers between devices, per_device(): kvs = lax.all_gather(kv, 'row', axis=0)  79.4 us
    pallas_call x1, Pallas kernels, row_call(): pl.pallas_call(row_kernel, grid=(tokens // tile,), in_specs=[full(x.shape...  35.1 us
    pallas_call x1, Pallas kernels, col_call(): pl.pallas_call(col_kernel, grid=(cols // per,), in_specs=[full(starts.sha...  33.7 us
    all_gather x1, blocking collectives, per_device(): every = lax.all_gather(mine, 'col', axis=0)  23 us
    pallas_call x1, Pallas kernels, conv_call(): pl.pallas_call(conv_kernel, grid=(fine_rows // step_rows,), in_specs=[ful...  13.4 us
    ppermute x2, starting transfers between devices, padded_2(): lax.ppermute(lax.slice_in_dim(block, 0, width, axis=dim), axis, backward)  6.29 us
    ppermute x2, starting transfers between devices, padded_2(): lax.ppermute(lax.slice_in_dim(block, block.shape[dim] - width, None, axis...  5.14 us
    ppermute x2, waiting for transfers between devices, padded_2(): lax.ppermute(lax.slice_in_dim(block, 0, width, axis=dim), axis, backward)  4.63 us
  transfers between devices with their start and end apart: 5, of which 3 were waited for; matrix products, arithmetic and copies ran while one was open for 1% of the time, Pallas kernels for 0%

profile of v1, /device:TPU:3, one launch (start us, length us, event | category | flops | bytes accessed | tf_op | source)
XLA Modules:
  0.0 226.8 jit_solution(8693170253993786654)
XLA Ops:
  7.2 0.0 all-gather.3.cloned.1.call-start
  7.2 1.4 convert_reduce_fusion
  8.6 23.0 %all-gather = f32[256,512]{1,0:T(8,128)S(1)} all-gather(f32[32,512]{1,0:T(8,128)S(1)} %convert_reduce_fusion), channel_id=2, replica_groups=mesh['row'=16,'col'=8] {'col'}, dimensions={0}, use_global_device_ids=true | all-gather | bytes 589824 | tf_op jit(solution)/shard_map/all_gather | solution.py:368
  31.6 1.3 pad.9.codes_ref
  32.9 0.7 select_reduce_fusion.base_ref
  33.7 35.1 %row_part.1 = (f32[2048,512]{1,0:T(8,128)}, bf16[2048,1024]{1,0:T(8,128)(2,1)}, bf16[2048,128]{1,0:T(8,128)(2,1)}) custom-call(s32[32,128]{1,0:T(8,128)} %pad.9.codes_ref, f32[32,512]{1,0:T(8,128)} %select_reduce_fusion.base_ref, bf16[512,512]{1,0:T(8,128)(2,1)} %embed_ref.1, f32[1,512]{1,0:T(1,128)} %bitcast.17, bf16[512,1536]{1,0:T(8,128)(2,1)} %wqkv_ref.1, ...), custom_call_target="tpu_custom_call" | custom-call | tf_op jit(solution)/shard_map/row_part/pallas_call | solution.py:122
  68.8 0.0 all-gather.3.cloned.1.call-update
  68.8 0.8 dynamic_slice.3
  69.6 0.6 pad_bitcast_fusion.starts_ref
  70.2 79.4 %all-gather.3.cloned.1.call-done.kv_ref = bf16[16,64,32,128]{3,2,1,0:T(8,128)(2,1)} async-done(((bf16[1,64,32,128]{3,2,1,0:T(8,128)(2,1)}), bf16[16,64,32,128]{3,2,1,0:T(8,128)(2,1)}) %all-gather.3.cloned.1.call-update) | async-done | bytes 8388624 | tf_op jit(solution)/shard_map/all_gather | solution.py:376
  149.6 33.7 %col_part.1 = (f32[32,64,512]{2,1,0:T(8,128)}, bf16[64,32,128]{2,1,0:T(8,128)(2,1)}) custom-call(s32[1,128]{1,0:T(1,128)} %pad_bitcast_fusion.starts_ref, bf16[64,32,1024]{2,1,0:T(8,128)(2,1)} %bitcast.14, bf16[16,64,32,128]{3,2,1,0:T(8,128)(2,1)} %all-gather.3.cloned.1.call-done.kv_ref, f32[2048,512]{1,0:T(8,128)} %get-tuple-element.9.ar_ref, ...), custom_call_target="tpu_custom_call" | custom-call | tf_op jit(solution)/shard_map/col_part/pallas_call | solution.py:207
  183.4 1.2 copy.21
  184.6 3.2 %collective-permute-start = (bf16[1,64,128]{2,1,0:T(8,128)(2,1)S(1)}, bf16[1,64,128]{2,1,0:T(8,128)(2,1)S(1)}, u32[]{:S(2)}, u32[]{:S(2)}) collective-permute-start(bf16[1,64,128]{2,1,0:T(8,128)(2,1)S(1)} %get-tuple-element.14), channel_id=1, source_target_pairs={{0,8},{8,16},{16,24},{24,32},{32,40},{40,48},{48,56},{56,64},{64,7... | collective-permute-start | bytes 49160 | tf_op jit(solution)/shard_map/ppermute | solution.py:352
  187.8 1.9 collective-permute-start.1
  189.8 0.0 collective-permute-done
  189.8 4.6 %collective-permute-done.1 = bf16[1,64,128]{2,1,0:T(8,128)(2,1)S(1)} collective-permute-done((bf16[1,64,128]{2,1,0:T(8,128)(2,1)S(1)}, bf16[1,64,128]{2,1,0:T(8,128)(2,1)S(1)}, u32[]{:S(2)}, u32[]{:S(2)}) %collective-permute-start.1) | collective-permute-done | bytes 16416 | tf_op jit(solution)/shard_map/ppermute | solution.py:355
  194.4 4.4 %collective-permute-start.2 = (bf16[34,1,128]{2,1,0:T(2,128)(2,1)S(1)}, bf16[34,1,128]{2,1,0:T(2,128)(2,1)S(1)}, u32[]{:S(2)}, u32[]{:S(2)}) collective-permute-start(bf16[34,1,128]{2,1,0:T(2,128)(2,1)S(1)} %get-tuple-element.12), channel_id=1, source_target_pairs={{1,0},{2,1},{3,2},{4,3},{5,4},{6,5},{7,6},{9,8},{10,9},{11,10},{12... | collective-permute-start | bytes 26120 | tf_op jit(solution)/shard_map/ppermute | solution.py:355
  198.8 1.9 collective-permute-start.3
  200.8 0.1 pad.14.clone
  200.8 0.0 collective-permute-done.2
  200.8 4.6 %collective-permute-done.3 = bf16[34,1,128]{2,1,0:T(2,128)(2,1)S(1)} collective-permute-done((bf16[34,1,128]{2,1,0:T(2,128)(2,1)S(1)}, bf16[34,1,128]{2,1,0:T(2,128)(2,1)S(1)}, u32[]{:S(2)}, u32[]{:S(2)}) %collective-permute-start.3) | collective-permute-done | bytes 8736 | tf_op jit(solution)/shard_map/ppermute | solution.py:352
  205.4 1.1 pad_maximum_fusion.ext_ref
  206.5 13.4 %conv_part.1 = f32[64,128,128]{2,1,0:T(8,128)} custom-call(bf16[34,80,128]{2,1,0:T(8,128)(2,1)} %pad_maximum_fusion.ext_ref, bf16[3,3,128,128]{3,2,1,0:T(8,128)(2,1)} %k1_ref.1, bf16[3,3,128,128]{3,2,1,0:T(8,128)(2,1)} %k2_ref.1), custom_call_target="tpu_custom_call" | custom-call | tf_op jit(solution)/shard_map/conv_part/pallas_call | solution.py:330
  (4 shorter events, 0.0 us)
Async XLA Ops:
  7.2 142.5 %all-gather.3.cloned.1.call-start = ((), (), s32[]{:S(2)}) async-start(), calls=%async_computation | async-start | bytes 8912896 | tf_op jit(solution)/shard_map/all_gather | solution.py:376
  184.6 5.2 %collective-permute-start = (bf16[1,64,128]{2,1,0:T(8,128)(2,1)S(1)}, bf16[1,64,128]{2,1,0:T(8,128)(2,1)S(1)}, u32[]{:S(2)}, u32[]{:S(2)}) collective-permute-start(bf16[1,64,128]{2,1,0:T(8,128)(2,1)S(1)} %get-tuple-element.14), channel_id=1, source_target_pairs={{0,8},{8,16},{16,24},{24,32},{32,40},{40,48},{48,56},{56,64},{64,7... | collective-permute-start | bytes 49160 | tf_op jit(solution)/shard_map/ppermute | solution.py:352
  187.8 6.6 %collective-permute-start.1 = (bf16[1,64,128]{2,1,0:T(8,128)(2,1)S(1)}, bf16[1,64,128]{2,1,0:T(8,128)(2,1)S(1)}, u32[]{:S(2)}, u32[]{:S(2)}) collective-permute-start(bf16[1,64,128]{2,1,0:T(8,128)(2,1)S(1)} %get-tuple-element.15), channel_id=1, source_target_pairs={{8,0},{16,8},{24,16},{32,24},{40,32},{48,40},{56,48},{64,56},{72,6... | collective-permute-start | bytes 49160 | tf_op jit(solution)/shard_map/ppermute | solution.py:355
  194.4 6.4 %collective-permute-start.2 = (bf16[34,1,128]{2,1,0:T(2,128)(2,1)S(1)}, bf16[34,1,128]{2,1,0:T(2,128)(2,1)S(1)}, u32[]{:S(2)}, u32[]{:S(2)}) collective-permute-start(bf16[34,1,128]{2,1,0:T(2,128)(2,1)S(1)} %get-tuple-element.12), channel_id=1, source_target_pairs={{1,0},{2,1},{3,2},{4,3},{5,4},{6,5},{7,6},{9,8},{10,9},{11,10},{12... | collective-permute-start | bytes 26120 | tf_op jit(solution)/shard_map/ppermute | solution.py:355
  198.8 6.6 %collective-permute-start.3 = (bf16[34,1,128]{2,1,0:T(2,128)(2,1)S(1)}, bf16[34,1,128]{2,1,0:T(2,128)(2,1)S(1)}, u32[]{:S(2)}, u32[]{:S(2)}) collective-permute-start(bf16[34,1,128]{2,1,0:T(2,128)(2,1)S(1)} %get-tuple-element.13), channel_id=1, source_target_pairs={{0,1},{1,2},{2,3},{3,4},{4,5},{5,6},{6,7},{8,9},{9,10},{10,11},{11... | collective-permute-start | bytes 26120 | tf_op jit(solution)/shard_map/ppermute | solution.py:352
Sparse Core Ops, SparseCore 0:
  68.9 80.6 all-gather.2

commit v2 on v1

v2 whole, which is shorter than its diff:
```python
import functools
import math
import jax
import jax.numpy as jnp
from jax import lax
from jax.experimental import pallas as pl
from jax.experimental.pallas import tpu as pltpu
from jax.sharding import PartitionSpec as P

HEADS = 8
HD = 64
EPS = 1e-06
NEGATIVE = -1e30
LOG2E = math.log2(math.e)
F32 = jnp.float32
BF16 = jnp.bfloat16
MESH = pl.DeviceIdType.MESH
VMEM_LIMIT = 56 * 1024 * 1024


def dot(left, right):
    return jnp.dot(left, right, preferred_element_type=F32)


def dot_t(left, right):
    return lax.dot_general(left, right, (((1,), (1,)), ((), ())), preferred_element_type=F32)


def norm_round(values, norm_gain):
    scale = lax.rsqrt(jnp.mean(values * values, axis=-1, keepdims=True) + EPS)
    return (values * scale * norm_gain).astype(BF16)


def silu(v):
    return v / (1.0 + jnp.exp(-v))


def lane_low(rows):
    return lax.broadcasted_iota(jnp.int32, (rows, 128), 1) < HD


PER = 8


def row_setup(embed_ref, g1_ref, wqkv_ref, wcol_ref, qtab, kz, vz, tri, wq2, rows):
    vocab, width = embed_ref.shape
    tile = tri.shape[0]
    scale = (HD ** -0.5) * LOG2E
    normed = norm_round(embed_ref[...].astype(F32), g1_ref[...])
    low = lane_low(vocab)
    qtab[...] = (dot(normed, wqkv_ref[:, :width]) * scale).astype(BF16)
    keys = dot(normed, wqkv_ref[:, width : 2 * width])
    values = dot(normed, wqkv_ref[:, 2 * width :])
    for h in range(HEADS):
        p = h // 2
        mine = low if h % 2 == 0 else jnp.logical_not(low)
        sl = slice(p * 128, p * 128 + 128)
        kz[h] = jnp.where(mine, keys[:, sl], 0.0).astype(BF16)
        vz[h] = jnp.where(mine, values[:, sl], 1.0).astype(BF16)
    out_t = lax.broadcasted_iota(jnp.int32, (tile, tile), 0)
    in_t = lax.broadcasted_iota(jnp.int32, (tile, tile), 1)
    tri[...] = jnp.where(
        (out_t % rows == in_t % rows) & (in_t // rows <= out_t // rows), 1.0, 0.0
    ).astype(BF16)
    lowd = lane_low(width)
    for p in range(HEADS // 2):
        w = wcol_ref[:, p * 128 : p * 128 + 128].astype(F32)
        wq2[:, (2 * p) * 128 : (2 * p + 1) * 128] = jnp.where(lowd, w, 0.0).astype(BF16)
        wq2[:, (2 * p + 1) * 128 : (2 * p + 2) * 128] = jnp.where(
            lowd, pltpu.roll(w, HD, 1), 0.0
        ).astype(BF16)


def row_tile(k, codes_ref, embed_ref, wro_ref, g2_ref, wcol_ref, qtab, kz, vz, seen, tri, wq2):
    vocab, width = embed_ref.shape
    rows = codes_ref.shape[0]
    tile = tri.shape[0]
    scale = (HD ** -0.5) * LOG2E
    rolled = pltpu.roll(codes_ref[...], 128 - PER * k, 1)
    ids = lax.broadcasted_iota(jnp.int32, (rows, vocab), 1)
    one_hot = jnp.concatenate(
        [jnp.where(rolled[:, c : c + 1] == ids, 1.0, 0.0) for c in range(PER)], axis=0
    ).astype(BF16)
    counts = dot(tri[...], one_hot) + jnp.concatenate([seen[...]] * PER, axis=0)
    seen[...] = counts[tile - rows :]
    logn = jnp.where(counts > 0.5, jnp.log2(jnp.maximum(counts, 1.0)), NEGATIVE)
    emb = dot(one_hot, embed_ref[...])
    q = dot(one_hot, qtab[...]).astype(BF16)
    low = lane_low(tile)
    mixed = []
    for p in range(HEADS // 2):
        outs = []
        qp = q[:, p * 128 : p * 128 + 128]
        for h in (2 * p, 2 * p + 1):
            s = dot_t(qp, kz[h]) + logn
            top = jnp.max(s, axis=-1, keepdims=True)
            e = jnp.exp2(s - top).astype(BF16)
            outs.append(dot(e, vz[h]))
        num = jnp.where(low, outs[0], outs[1])
        den = pltpu.roll(jnp.where(low, outs[1], outs[0]), HD, 1)
        mixed.append((num / den).astype(BF16))
    after = emb + dot(jnp.concatenate(mixed, axis=1), wro_ref[...])
    normed = norm_round(after, g2_ref[...])
    q2 = dot(normed, wq2[...]) * scale
    lane = lax.broadcasted_iota(jnp.int32, (tile, 128), 1)
    row = lax.broadcasted_iota(jnp.int32, (tile, 128), 0) % rows
    mark = jnp.where(lane == HD + row, 1.0, 0.0)
    q2 = jnp.concatenate(
        [(q2[:, h * 128 : h * 128 + 128] + mark).astype(BF16) for h in range(HEADS)], axis=1
    )
    return after, q2, dot(normed, wcol_ref[:, width:]).astype(BF16)


def set_bias(bias, starts_ref, first):
    lane = lax.broadcasted_iota(jnp.int32, bias.shape, 1)
    key_row = lax.broadcasted_iota(jnp.int32, bias.shape, 0)
    query_row = first + lane - HD
    seen = (key_row <= query_row) & (key_row >= starts_ref[0:1, :])
    bias[...] = jnp.where((lane < HD) | seen, 0.0, NEGATIVE).astype(BF16)


def col_tile(q_of, kv_of, bias, mixed, rows, keys):
    low_f = jnp.where(lane_low(keys), 1.0, 0.0)
    low_k = low_f.astype(BF16)
    high_k = (1.0 - low_f).astype(BF16)
    low = lane_low(rows)
    for c in range(PER):
        kv = kv_of(c)
        ka = kv * low_k + bias[...]
        va = kv * high_k + low_k
        q = q_of(c)
        q = jnp.concatenate([q[:, h * 128 : h * 128 + 128] for h in range(HEADS)], axis=0)
        s = dot_t(q, ka)
        top = jnp.max(s, axis=-1, keepdims=True)
        e = jnp.exp2(s - top).astype(BF16)
        o = dot(e, va)
        for p in range(HEADS // 2):
            even = o[(2 * p) * rows : (2 * p + 1) * rows]
            odd = o[(2 * p + 1) * rows : (2 * p + 2) * rows]
            keep = jnp.where(low, even, odd)
            other = pltpu.roll(jnp.where(low, odd, even), HD, 1)
            num = jnp.where(low, other, keep)
            den = jnp.where(low, keep, other)
            mixed[c * rows : (c + 1) * rows, p * 128 : p * 128 + 128] = (num / den).astype(BF16)


CORNERS = ((-1, -1), (-1, 1), (1, -1), (1, 1))


def front_kernel(
    row_count, col_count,
    codes_ref, starts_ref, embed_ref, g1_ref, wqkv_ref, wro_ref, g2_ref, wcol_ref, wco_ref,
    after_ref, halo_ref,
    qtab, kz, vz, seen, tri, wq2, bias, mixed, kv_all, q2_all, held, hist, edge,
    kv_send, kv_recv, hist_send, hist_recv, halo_send, halo_recv, out_sem,
):
    rows = codes_ref.shape[0]
    vocab, width = embed_ref.shape
    slots, cols = kv_all.shape[0], kv_all.shape[1]
    keys = slots * rows
    tile = PER * rows
    chunks = cols // PER
    my_row, my_col = lax.axis_index("row"), lax.axis_index("col")

    half = row_count // 4

    def sibling(r):
        return r + 1 - 2 * lax.rem(r, 2)

    def across(r):
        return r + 2 - 4 * lax.rem(lax.div(r, 2), 2)

    def turned(r, steps):
        return lax.rem(r + 4 * steps, row_count)

    sib, beyond = sibling(my_row), across(my_row)
    down, up = turned(my_row, 1), turned(my_row, half - 1)
    far = turned(my_row, 2)

    halo_ref[...] = jnp.zeros_like(halo_ref)
    def row_by(dr):
        return lax.rem(my_row + dr + row_count, row_count)

    barrier = pltpu.get_barrier_semaphore()
    other = row_by(2 * lax.rem(my_row, 2) - 1)
    peers = [{"row": r, "col": my_col} for r in (sib, beyond, down, up, other)]
    for d in range(1, col_count):
        peers.append({"row": my_row, "col": lax.rem(my_col + d, col_count)})
    for dr, dc in CORNERS:
        peers.append({"row": row_by(dr), "col": lax.rem(my_col + dc + col_count, col_count)})
    for peer in peers:
        pl.semaphore_signal(barrier, 1, device_id=peer, device_id_type=MESH)

    def there(dr, dc):
        ok = None
        for at, step, count in ((my_row, dr, row_count), (my_col, dc, col_count)):
            if step:
                t = at + step >= 0 if step < 0 else at + step < count
                ok = t if ok is None else ok & t
        return ok

    ids = lax.broadcasted_iota(jnp.int32, (rows, vocab), 1)
    codes = codes_ref[...]
    own = jnp.zeros((rows, vocab), F32)
    for c in range(cols):
        own = own + jnp.where(codes[:, c : c + 1] == ids, 1.0, 0.0)
    hist[my_col] = own.astype(BF16)

    pl.semaphore_wait(barrier, len(peers))

    def hist_copy(d, slot):
        return pltpu.make_async_remote_copy(
            src_ref=hist.at[slot], dst_ref=hist.at[slot],
            send_sem=hist_send.at[d], recv_sem=hist_recv.at[slot],
            device_id={"col": lax.rem(my_col + d, col_count)}, device_id_type=MESH,
        )

    for d in range(1, col_count):
        hist_copy(d, my_col).start()

    row_setup(embed_ref, g1_ref, wqkv_ref, wcol_ref, qtab, kz, vz, tri, wq2, rows)
    set_bias(bias, starts_ref, my_row * rows)

    for d in range(1, col_count):
        hist_copy(d, lax.rem(my_col + d, col_count)).wait_recv()
    base = jnp.zeros((rows, vocab), F32)
    for c in range(col_count):
        base = base + jnp.where(c < my_col, 1.0, 0.0) * hist[c].astype(F32)
    seen[...] = base

    def kv_copy(n, k, slot, dest):
        part = kv_all.at[slot, pl.ds(k * PER, PER)]
        return pltpu.make_async_remote_copy(
            src_ref=part, dst_ref=part,
            send_sem=kv_send.at[n, k], recv_sem=kv_recv.at[slot, k],
            device_id={"row": dest}, device_id_type=MESH,
        )

    def arrived(k, slot):
        kv_copy(0, k, slot, sib).wait_recv()

    def relay(s):
        k1 = s - 1

        @pl.when((k1 >= 0) & (k1 < chunks))
        def _():
            arrived(k1, beyond)
            kv_copy(4, k1, beyond, down).start()
            kv_copy(5, k1, beyond, up).start()
            kv_copy(6, k1, beyond, sib).start()

        k2 = s - 2

        @pl.when((k2 >= 0) & (k2 < chunks))
        def _():
            from_up = (up, turned(beyond, half - 1))
            from_down = (down, turned(beyond, 1))
            for i, slot in enumerate(from_up + from_down):
                arrived(k2, slot)
            even = lax.rem(k2, 2) == 0
            for i in range(2):
                @pl.when(even)
                def _():
                    kv_copy(7 + i, k2, from_up[i], down).start()

                @pl.when(jnp.logical_not(even))
                def _():
                    kv_copy(7 + i, k2, from_down[i], up).start()
            for i, slot in enumerate(from_up + from_down):
                kv_copy(9 + i, k2, slot, sib).start()

        k3 = s - 3

        @pl.when((k3 >= 0) & (k3 < chunks))
        def _():
            for i, slot in enumerate((far, turned(beyond, 2))):
                arrived(k3, slot)
                kv_copy(13 + i, k3, slot, sib).start()

    def row_step(k, carry):
        relay(k)
        after, q2, kv = row_tile(
            k, codes_ref, embed_ref, wro_ref, g2_ref, wcol_ref, qtab, kz, vz, seen, tri, wq2
        )
        kv_all[my_row, pl.ds(k * PER, PER)] = kv.reshape(PER, rows, 2 * HD)
        kv_copy(0, k, my_row, beyond).start()
        kv_copy(1, k, my_row, down).start()
        kv_copy(2, k, my_row, up).start()
        kv_copy(3, k, my_row, sib).start()
        held[pl.ds(k * tile, tile)] = after
        q2_all[pl.ds(k * PER, PER)] = q2.reshape(PER, rows, 2 * width)
        return carry

    lax.fori_loop(0, chunks, row_step, 0)

    def halo_copy(sem, src, at, size, dr, dc):
        return pltpu.make_async_remote_copy(
            src_ref=src, dst_ref=halo_ref.at[pl.ds(at, size)],
            send_sem=halo_send.at[sem], recv_sem=halo_recv.at[sem],
            device_id={"row": my_row + dr, "col": my_col + dc}, device_id_type=MESH,
        )

    left_at, corner_at = 2 * cols, 2 * cols + 2 * rows
    side_sem = 2 * chunks

    def edge_copy(which, k, dr):
        at = cols if which == 0 else 0
        return halo_copy(
            which * chunks + k, edge.at[which, pl.ds(k * PER, PER)], at + k * PER, PER, dr, 0
        )

    def side_copy(which, dc):
        c = 0 if which == 0 else cols - 1
        at = left_at + rows if which == 0 else left_at
        return halo_copy(side_sem + which, held.at[pl.ds(c * rows, rows)], at, rows, 0, dc)

    def corner_copy(i, dr, dc):
        k = 0 if dc < 0 else chunks - 1
        at = corner_at + (len(CORNERS) - 1 - i) * PER
        return halo_copy(
            side_sem + 2 + i, edge.at[0 if dr < 0 else 1, pl.ds(k * PER, PER)], at, PER, dr, dc
        )

    def out_copy(k):
        return pltpu.make_async_copy(
            held.at[pl.ds(k * tile, tile)], after_ref.at[pl.ds(k * tile, tile)], out_sem.at[k]
        )

    def col_step(j, carry):
        relay(chunks + j)
        mid = chunks // 2
        k = jnp.where(j < mid, j, jnp.where(j == mid, chunks - 1, j - 1))
        for slot in (
            my_row, beyond, down, turned(beyond, 1), up, turned(beyond, half - 1),
            far, turned(beyond, 2),
        ):
            arrived(k, sibling(slot))
        col_tile(
            lambda c: q2_all[k * PER + c],
            lambda c: kv_all[:, k * PER + c].reshape(keys, 2 * HD),
            bias, mixed, rows, keys,
        )
        after = held[pl.ds(k * tile, tile)] + dot(mixed[...], wco_ref[...])
        held[pl.ds(k * tile, tile)] = after
        out_copy(k).start()
        grid = after.reshape(PER, rows, width)
        edge[0, pl.ds(k * PER, PER)] = grid[:, 0]
        edge[1, pl.ds(k * PER, PER)] = grid[:, rows - 1]

        @pl.when(there(-1, 0))
        def _():
            edge_copy(0, k, -1).start()

        @pl.when(there(1, 0))
        def _():
            edge_copy(1, k, 1).start()

        for which, dc in ((0, -1), (1, 1)):
            last = 0 if which == 0 else chunks - 1

            @pl.when(there(0, dc) & (k == last))
            def _():
                side_copy(which, dc).start()

        for i, (dr, dc) in enumerate(CORNERS):
            last = 0 if dc < 0 else chunks - 1

            @pl.when(there(dr, dc) & (k == last))
            def _():
                corner_copy(i, dr, dc).start()

        return carry

    lax.fori_loop(0, chunks, col_step, 0)

    for d in range(1, col_count):
        hist_copy(d, my_col).wait_send()

    def finish(k, carry):
        for n in range(kv_send.shape[0]):
            kv_copy(n, k, my_row, sib).wait_send()
        out_copy(k).wait()

        @pl.when(there(-1, 0))
        def _():
            edge_copy(0, k, -1).wait_send()
            edge_copy(1, k, -1).wait_recv()

        @pl.when(there(1, 0))
        def _():
            edge_copy(1, k, 1).wait_send()
            edge_copy(0, k, 1).wait_recv()

        return carry

    lax.fori_loop(0, chunks, finish, 0)
    for which, dc in ((0, -1), (1, 1)):
        @pl.when(there(0, dc))
        def _():
            side_copy(which, dc).wait_send()
            side_copy(1 - which, dc).wait_recv()
    for i, (dr, dc) in enumerate(CORNERS):
        @pl.when(there(dr, dc))
        def _():
            corner_copy(i, dr, dc).wait_send()
            corner_copy(len(CORNERS) - 1 - i, dr, dc).wait_recv()


def full(shape):
    return pl.BlockSpec(shape, lambda *_: (0,) * len(shape))


def front_call(codes, starts, embed, g1, wqkv, wro, g2, wcol, wco, cols):
    vocab, width = embed.shape
    rows = codes.shape[0]
    row_count, col_count = lax.axis_size("row"), lax.axis_size("col")
    tokens = rows * cols
    tile = rows * PER
    chunks = cols // PER
    halo = -(-(2 * cols + 2 * rows + 4 * PER) // tile) * tile
    dma = pltpu.SemaphoreType.DMA
    args = (codes, starts, embed, g1, wqkv, wro, g2, wcol, wco)
    return pl.pallas_call(
        functools.partial(front_kernel, row_count, col_count),
        in_specs=[pl.BlockSpec(memory_space=pltpu.VMEM)] * len(args),
        out_specs=[
            pl.BlockSpec(memory_space=pl.ANY),
            pl.BlockSpec(memory_space=pltpu.VMEM),
        ],
        out_shape=[
            jax.ShapeDtypeStruct((tokens, width), F32),
            jax.ShapeDtypeStruct((halo, width), F32),
        ],
        scratch_shapes=[
            pltpu.VMEM((vocab, width), BF16),
            pltpu.VMEM((HEADS, vocab, 128), BF16),
            pltpu.VMEM((HEADS, vocab, 128), BF16),
            pltpu.VMEM((rows, vocab), F32),
            pltpu.VMEM((tile, tile), BF16),
            pltpu.VMEM((width, 2 * width), BF16),
            pltpu.VMEM((row_count * rows, 128), BF16),
            pltpu.VMEM((tile, width), BF16),
            pltpu.VMEM((row_count, cols, rows, 2 * HD), BF16),
            pltpu.VMEM((cols, rows, 2 * width), BF16),
            pltpu.VMEM((tokens, width), F32),
            pltpu.VMEM((col_count, rows, vocab), BF16),
            pltpu.VMEM((2, cols, width), F32),
            dma((15, chunks)),
            dma((row_count, chunks)),
            dma((col_count,)),
            dma((col_count,)),
            dma((2 * chunks + 6,)),
            dma((2 * chunks + 6,)),
            dma((chunks,)),
        ],
        compiler_params=pltpu.CompilerParams(
            vmem_limit_bytes=VMEM_LIMIT, collective_id=0, has_side_effects=True
        ),
        name="front",
    )(*args)


def back_kernel(
    col_steps,
    after_ref, halo_ref, g3_ref, win_ref, wout_ref, wp_ref, k1_ref, k2_ref,
    bo_ref, img_ref,
    ext, w1, w2, cat, fine,
):
    k = pl.program_id(0)
    erows, ring, ch = ext.shape
    rows = erows - 2
    pairs = erows - 1
    cols = img_ref.shape[1] // 2
    fine_step = img_ref.shape[0]
    my_row, my_col = lax.axis_index("row"), lax.axis_index("col")
    at_top, at_bottom = my_row == 0, my_row == lax.axis_size("row") - 1
    at_left, at_right = my_col == 0, my_col == lax.axis_size("col") - 1

    def cells(after):
        normed = norm_round(after, g3_ref[...])
        inner = silu(dot(normed, win_ref[...])).astype(BF16)
        out = after + dot(inner, wout_ref[...])
        coarse = dot(out.astype(BF16), wp_ref[...]).astype(BF16).astype(F32)
        return out, coarse

    @pl.when(k == 0)
    def _():
        ext[...] = jnp.zeros_like(ext)

    @pl.when(k < col_steps)
    def _():
        out, coarse = cells(after_ref[...])
        bo_ref[...] = jnp.swapaxes(out.reshape(PER, rows, out.shape[1]), 0, 1)
        at = pl.multiple_of(k * PER, PER)
        ext[1 : rows + 1, pl.ds(at, PER), :] = jnp.swapaxes(coarse.reshape(PER, rows, ch), 0, 1)

    @pl.when(k == col_steps)
    def _():
        _, coarse = cells(halo_ref[...])
        zero = jnp.float32(0.0)
        ext[0, 0:cols] = jnp.where(at_top, zero, coarse[0:cols])
        ext[rows + 1, 0:cols] = jnp.where(at_bottom, zero, coarse[cols : 2 * cols])
        left = coarse[2 * cols : 2 * cols + rows]
        right = coarse[2 * cols + rows : 2 * cols + 2 * rows]
        ext[1 : rows + 1, ring - 1 : ring, :] = jnp.where(at_left, zero, left).reshape(rows, 1, ch)
        ext[1 : rows + 1, cols : cols + 1, :] = jnp.where(at_right, zero, right).reshape(rows, 1, ch)
        for i, (dr, dc) in enumerate(CORNERS):
            at = 2 * cols + 2 * rows + i * PER + (PER - 1 if dc < 0 else 0)
            outside = (at_top if dr < 0 else at_bottom) | (at_left if dc < 0 else at_right)
            to_row = 0 if dr < 0 else rows + 1
            to_col = ring - 1 if dc < 0 else cols
            ext[to_row, to_col : to_col + 1, :] = jnp.where(outside, zero, coarse[at : at + 1])
        taps = [[k1_ref[y, x].astype(F32) for x in range(3)] for y in range(3)]
        none = jnp.zeros((ch, ch), F32)
        by_half = (
            ([taps[0][x] + taps[1][x] for x in range(3)], taps[2]),
            (taps[0], [taps[1][x] + taps[2][x] for x in range(3)]),
        )
        for half in range(2):
            for dy in range(2):
                t = by_half[half][dy]
                for b in range(2):
                    three = (t[0], t[1] + t[2], none) if b == 0 else (none, t[0] + t[1], t[2])
                    for dx in range(3):
                        w1[
                            (dy * 3 + dx) * ch : (dy * 3 + dx + 1) * ch,
                            (half * 2 + b) * ch : (half * 2 + b + 1) * ch,
                        ] = three[dx].astype(BF16)
        for dy in range(3):
            for s in range(4):
                for b in range(2):
                    w2[(dy * 4 + s) * ch : (dy * 4 + s + 1) * ch, b * ch : (b + 1) * ch] = (
                        k2_ref[dy, s - b] if 0 <= s - b <= 2 else none.astype(BF16)
                    )

        def widen(e, carry):
            x = ext[e]
            cat[e] = jnp.concatenate(
                [pltpu.roll(x, 1, 0), x, pltpu.roll(x, ring - 1, 0)], axis=1
            ).astype(BF16)
            return carry

        lax.fori_loop(0, erows, widen, 0)
        place = lax.broadcasted_iota(jnp.int32, (ring, 128), 0)
        col_keep = jnp.where(
            ((place == ring - 1) & at_left) | ((place == cols) & at_right), 0.0, 1.0
        )
        group = 3

        def first_conv(g, carry):
            e0 = g * group
            left = jnp.concatenate(
                [
                    jnp.concatenate([cat[e0 + i], cat[e0 + i + 1]], axis=1)
                    for i in range(group)
                ],
                axis=0,
            )
            y = silu(dot(left, w1[...]))
            for i in range(group):
                for half in range(2):
                    f = 2 * (e0 + i) + half
                    outside = ((f == 0) & at_top) | ((f == 2 * pairs - 1) & at_bottom)
                    keep = jnp.where(outside, 0.0, 1.0) * col_keep
                    f0 = y[i * ring : (i + 1) * ring, (2 * half) * ch : (2 * half + 1) * ch] * keep
                    f1 = y[i * ring : (i + 1) * ring, (2 * half + 1) * ch : (2 * half + 2) * ch] * keep
                    fine[f] = jnp.concatenate(
                        [pltpu.roll(f1, 1, 0), f0, f1, pltpu.roll(f0, ring - 1, 0)], axis=1
                    ).astype(BF16)
            return carry

        lax.fori_loop(0, pairs // group, first_conv, 0)

    @pl.when(k > col_steps)
    def _():
        m = k - col_steps - 1
        y0 = m * fine_step
        left = jnp.concatenate(
            [
                jnp.concatenate([fine[y0 + i + dy, 0:cols] for dy in range(3)], axis=1)
                for i in range(fine_step)
            ],
            axis=0,
        )
        second = dot(left, w2[...])
        for i in range(fine_step):
            up = ext[m * (fine_step // 2) + i // 2 + 1, 0:cols]
            for b in range(2):
                img_ref[i, pl.ds(b, cols, stride=2), :] = (
                    second[i * cols : (i + 1) * cols, b * ch : (b + 1) * ch] + up
                )


def back_call(after, halo, g3, win, wout, wp, k1, k2, rows, cols):
    width = after.shape[1]
    ch = wp.shape[1]
    tile = rows * PER
    col_steps = cols // PER
    ring = cols + 16
    fine_step = 8
    return pl.pallas_call(
        functools.partial(back_kernel, col_steps),
        grid=(col_steps + 1 + 2 * rows // fine_step,),
        in_specs=[pl.BlockSpec((tile, width), lambda i: (jnp.minimum(i, col_steps - 1), 0))]
        + [full(x.shape) for x in (halo, g3, win, wout, wp, k1, k2)],
        out_specs=[
            pl.BlockSpec((rows, PER, width), lambda i: (0, jnp.minimum(i, col_steps - 1), 0)),
            pl.BlockSpec(
                (fine_step, 2 * cols, ch), lambda i: (jnp.maximum(i - col_steps - 1, 0), 0, 0)
            ),
        ],
        out_shape=[
            jax.ShapeDtypeStruct((rows, cols, width), F32),
            jax.ShapeDtypeStruct((2 * rows, 2 * cols, ch), F32),
        ],
        scratch_shapes=[
            pltpu.VMEM((rows + 2, ring, ch), F32),
            pltpu.VMEM((6 * ch, 4 * ch), BF16),
            pltpu.VMEM((12 * ch, 2 * ch), BF16),
            pltpu.VMEM((rows + 2, ring, 3 * ch), BF16),
            pltpu.VMEM((2 * rows + 2, ring, 4 * ch), BF16),
        ],
        compiler_params=pltpu.CompilerParams(vmem_limit_bytes=VMEM_LIMIT),
        name="back",
    )(after, halo, g3, win, wout, wp, k1, k2)


def per_device(
    codes, starts, embed, gain_one, row_qkv, row_out, gain_two, col_qkv, col_out,
    gain_three, mlp_in, mlp_out, project, conv_one, conv_two,
):
    rows, cols = codes.shape
    wide = jnp.pad(codes, ((0, 0), (0, 128 - cols)))
    my_starts = lax.dynamic_slice_in_dim(starts, lax.axis_index("row") * rows, rows)
    my_starts = jnp.pad(my_starts, (HD, 128 - HD - rows))[None]
    after_col, halo = front_call(
        wide, my_starts, embed, gain_one[None], row_qkv, row_out, gain_two[None],
        col_qkv, col_out, cols,
    )
    return tuple(
        back_call(
            after_col, halo, gain_three[None], mlp_in, mlp_out, project, conv_one, conv_two,
            rows, cols,
        )
    )


def solution(mesh):
    in_specs = (P("row", "col"),) + (P(),) * 14
    out_specs = (P("row", "col", None), P("row", "col", None))
    return jax.shard_map(
        per_device, mesh=mesh, in_specs=in_specs, out_specs=out_specs, check_vma=False
    )
```

time: 228 us -> 140 us (0.61)
  waiting for transfers between devices: 88.7 us -> 0 us
  Pallas kernels: 82.2 us -> 134 us
  blocking collectives: 23 us -> 0 us
  between operations: 14.1 us -> 0.64 us
  starting transfers between devices: 11.5 us -> 0 us
  other arithmetic: 3.2 us -> 0 us
    all_gather x1 -> x0, waiting for transfers between devices: 79.4 us -> none  [per_device(): kvs = lax.all_gather(kv, 'row', axis=0)]
    pallas_call x3 -> x2, Pallas kernels: 82.2 us -> 134 us  [the longest x1 109 us: front_call(): pl.pallas_call(functools.partial(front_kernel, row_count, col_count), in_...]
    all_gather x1 -> x0, blocking collectives: 23 us -> none  [per_device(): every = lax.all_gather(mine, 'col', axis=0)]
    ppermute x4 -> x0, starting transfers between devices: 11.4 us -> none  [the longest x2 6.29 us: padded_2(): lax.ppermute(lax.slice_in_dim(block, 0, width, axis=dim), axis, backward)]
    ppermute x4 -> x0, waiting for transfers between devices: 9.21 us -> none  [the longest x2 4.63 us: padded_2(): lax.ppermute(lax.slice_in_dim(block, 0, width, axis=dim), axis, backward)]
  transfers between devices with their start and end apart: 5 -> 0, of which waited for: 3 -> 0; matrix products, arithmetic and copies ran while one was open for 1% -> 0% of each run, Pallas kernels for 0% -> 0%
where the time goes in v2:
time: 140 us; the launch traced here: 137 us
  Pallas kernels  134 us (96%)
  local copies, waits for them, and re-layouts  2.67 us (2%)
    pallas_call x1, Pallas kernels, front_call(): pl.pallas_call(functools.partial(front_kernel, row_count, col_count), in_...  109 us
    pallas_call x1, Pallas kernels, back_call(): pl.pallas_call(functools.partial(back_kernel, col_steps), grid=(col_steps...  24.5 us

profile of v2, /device:TPU:3, one launch (start us, length us, event | category | flops | bytes accessed | tf_op | source)
XLA Modules:
  0.0 137.3 jit_solution(15188449784815739141)
XLA Ops:
  0.6 0.8 dynamic_slice.3
  1.4 0.6 pad_bitcast_fusion.starts_ref
  2.0 1.3 pad.8.codes_ref
  3.3 109.4 %front.1 = (f32[2048,512]{1,0:T(8,128)}, f32[256,512]{1,0:T(8,128)}) custom-call(s32[32,128]{1,0:T(8,128)} %pad.8.codes_ref, s32[1,128]{1,0:T(1,128)} %pad_bitcast_fusion.starts_ref, bf16[512,512]{1,0:T(8,128)(2,1)} %embed_ref.1, f32[1,512]{1,0:T(1,128)} %bitcast.5, bf16[512,1536]{1,0:T(8,128)(2,1)} %wqkv_ref.1, bf16[512,512]{1,0:T(8,128)(2,1)} %wro_ref.1, ...), custom_call_target="tpu_custom_call" | custom-call | tf_op jit(solution)/shard_map/front/pallas_call | solution.py:423
  112.8 24.5 %back.1 = (f32[32,64,512]{2,1,0:T(8,128)}, f32[64,128,128]{2,1,0:T(8,128)}) custom-call(f32[2048,512]{1,0:T(8,128)} %get-tuple-element.4.after_ref, f32[256,512]{1,0:T(8,128)} %get-tuple-element.5.halo_ref, f32[1,512]{1,0:T(1,128)} %bitcast.7, bf16[512,1024]{1,0:T(8,128)(2,1)} %win_ref.1, bf16[1024,512]{1,0:T(8,128)(2,1)} %wout_ref.1, ...), custom_call_target="tpu_custom_call" | custom-call | tf_op jit(solution)/shard_map/back/pallas_call | solution.py:601

commit v3 on v2

--- a/solution.py
+++ b/solution.py
@@ -40,6 +40,7 @@
 
 
 PER = 8
+AHEAD = 2
 
 
 def row_setup(embed_ref, g1_ref, wqkv_ref, wcol_ref, qtab, kz, vz, tri, wq2, rows):
@@ -87,18 +88,24 @@
     emb = dot(one_hot, embed_ref[...])
     q = dot(one_hot, qtab[...]).astype(BF16)
     low = lane_low(tile)
-    mixed = []
-    for p in range(HEADS // 2):
-        outs = []
-        qp = q[:, p * 128 : p * 128 + 128]
-        for h in (2 * p, 2 * p + 1):
-            s = dot_t(qp, kz[h]) + logn
-            top = jnp.max(s, axis=-1, keepdims=True)
-            e = jnp.exp2(s - top).astype(BF16)
-            outs.append(dot(e, vz[h]))
-        num = jnp.where(low, outs[0], outs[1])
-        den = pltpu.roll(jnp.where(low, outs[1], outs[0]), HD, 1)
-        mixed.append((num / den).astype(BF16))
+
+    def scores(h):
+        return dot_t(q[:, h // 2 * 128 : h // 2 * 128 + 128], kz[h]) + logn
+
+    line = [scores(h) for h in range(AHEAD)]
+    mixed, outs = [], []
+    for h in range(HEADS):
+        s = line.pop(0)
+        if h + AHEAD < HEADS:
+            line.append(scores(h + AHEAD))
+        top = jnp.max(s, axis=-1, keepdims=True)
+        e = jnp.exp2(s - top).astype(BF16)
+        outs.append(dot(e, vz[h]))
+        if h % 2:
+            num = jnp.where(low, outs[0], outs[1])
+            den = pltpu.roll(jnp.where(low, outs[1], outs[0]), HD, 1)
+            mixed.append((num / den).astype(BF16))
+            outs = []
     after = emb + dot(jnp.concatenate(mixed, axis=1), wro_ref[...])
     normed = norm_round(after, g2_ref[...])
     q2 = dot(normed, wq2[...]) * scale
@@ -111,9 +118,11 @@
     return after, q2, dot(normed, wcol_ref[:, width:]).astype(BF16)
 
 
-def set_bias(bias, starts_ref, first):
+def set_bias(bias, starts_ref, first, rows):
     lane = lax.broadcasted_iota(jnp.int32, bias.shape, 1)
-    key_row = lax.broadcasted_iota(jnp.int32, bias.shape, 0)
+    place = lax.broadcasted_iota(jnp.int32, bias.shape, 0)
+    slot, line = place // rows, bias.shape[0] // rows // 2
+    key_row = ((slot % line) * 2 + slot // line) * rows + place % rows
     query_row = first + lane - HD
     seen = (key_row <= query_row) & (key_row >= starts_ref[0:1, :])
     bias[...] = jnp.where((lane < HD) | seen, 0.0, NEGATIVE).astype(BF16)
@@ -124,13 +133,18 @@
     low_k = low_f.astype(BF16)
     high_k = (1.0 - low_f).astype(BF16)
     low = lane_low(rows)
-    for c in range(PER):
+
+    def scores(c):
         kv = kv_of(c)
-        ka = kv * low_k + bias[...]
-        va = kv * high_k + low_k
         q = q_of(c)
         q = jnp.concatenate([q[:, h * 128 : h * 128 + 128] for h in range(HEADS)], axis=0)
-        s = dot_t(q, ka)
+        return dot_t(q, kv * low_k + bias[...]), kv * high_k + low_k
+
+    line = [scores(c) for c in range(AHEAD)]
+    for c in range(PER):
+        s, va = line.pop(0)
+        if c + AHEAD < PER:
+            line.append(scores(c + AHEAD))
         top = jnp.max(s, axis=-1, keepdims=True)
         e = jnp.exp2(s - top).astype(BF16)
         o = dot(e, va)
@@ -144,6 +158,7 @@
             mixed[c * rows : (c + 1) * rows, p * 128 : p * 128 + 128] = (num / den).astype(BF16)
 
 
+PAIRED = (5, 8, 9, 10)
 CORNERS = ((-1, -1), (-1, 1), (1, -1), (1, 1))
 
 
@@ -219,7 +234,7 @@
         hist_copy(d, my_col).start()
 
     row_setup(embed_ref, g1_ref, wqkv_ref, wcol_ref, qtab, kz, vz, tri, wq2, rows)
-    set_bias(bias, starts_ref, my_row * rows)
+    set_bias(bias, starts_ref, my_row * rows, rows)
 
     for d in range(1, col_count):
         hist_copy(d, lax.rem(my_col + d, col_count)).wait_recv()
@@ -228,65 +243,76 @@
         base = base + jnp.where(c < my_col, 1.0, 0.0) * hist[c].astype(F32)
     seen[...] = base
 
-    def kv_copy(n, k, slot, dest):
-        part = kv_all.at[slot, pl.ds(k * PER, PER)]
+    def slot_of(r):
+        return lax.rem(r, 2) * (slots // 2) + lax.div(r, 2)
+
+    def kv_copy(n, k, r, dest):
+        paired = n in PAIRED
+        slot = slot_of(r)
+        if paired:
+            slot = slot - lax.rem(slot, 2)
+        part = kv_all.at[pl.ds(slot, 2 if paired else 1), pl.ds(k * PER, PER)]
+        sem = slots + lax.div(slot, 2) if paired else slot
         return pltpu.make_async_remote_copy(
             src_ref=part, dst_ref=part,
-            send_sem=kv_send.at[n, k], recv_sem=kv_recv.at[slot, k],
+            send_sem=kv_send.at[n, k], recv_sem=kv_recv.at[sem, k],
             device_id={"row": dest}, device_id_type=MESH,
         )
 
-    def arrived(k, slot):
-        kv_copy(0, k, slot, sib).wait_recv()
+    def arrived(k, r, n=0):
+        kv_copy(n, k, r, sib).wait_recv()
+
+    up_beyond, down_beyond, far_beyond = across(up), across(down), across(far)
 
     def relay(s):
-        k1 = s - 1
+        k1 = s - 2
 
         @pl.when((k1 >= 0) & (k1 < chunks))
         def _():
             arrived(k1, beyond)
-            kv_copy(4, k1, beyond, down).start()
-            kv_copy(5, k1, beyond, up).start()
-            kv_copy(6, k1, beyond, sib).start()
-
-        k2 = s - 2
-
-        @pl.when((k2 >= 0) & (k2 < chunks))
-        def _():
-            from_up = (up, turned(beyond, half - 1))
-            from_down = (down, turned(beyond, 1))
-            for i, slot in enumerate(from_up + from_down):
-                arrived(k2, slot)
-            even = lax.rem(k2, 2) == 0
-            for i in range(2):
-                @pl.when(even)
-                def _():
-                    kv_copy(7 + i, k2, from_up[i], down).start()
-
-                @pl.when(jnp.logical_not(even))
-                def _():
-                    kv_copy(7 + i, k2, from_down[i], up).start()
-            for i, slot in enumerate(from_up + from_down):
-                kv_copy(9 + i, k2, slot, sib).start()
-
-        k3 = s - 3
+            kv_copy(3, k1, beyond, down).start()
+            kv_copy(4, k1, beyond, up).start()
+            kv_copy(5, k1, my_row, sib).start()
+            arrived(k1, up)
+            arrived(k1, down)
+            even = lax.rem(k1, 2) == 0
+
+            @pl.when(even)
+            def _():
+                kv_copy(6, k1, up, down).start()
+
+            @pl.when(jnp.logical_not(even))
+            def _():
+                kv_copy(6, k1, down, up).start()
+
+        mid = chunks // 2
+        k2 = jnp.where(s < mid + 4, s - 3, s - 4)
+
+        @pl.when((k2 >= 0) & (k2 < chunks) & (s != mid + 4))
+        def _():
+            arrived(k2, far)
+            kv_copy(7, k2, far, beyond).start()
+            arrived(k2, up_beyond)
+            kv_copy(8, k2, up, sib).start()
+            arrived(k2, down_beyond)
+            kv_copy(9, k2, down, sib).start()
+
+        k3 = s - 5
 
         @pl.when((k3 >= 0) & (k3 < chunks))
         def _():
-            for i, slot in enumerate((far, turned(beyond, 2))):
-                arrived(k3, slot)
-                kv_copy(13 + i, k3, slot, sib).start()
+            arrived(k3, far_beyond)
+            kv_copy(10, k3, far, sib).start()
 
     def row_step(k, carry):
         relay(k)
         after, q2, kv = row_tile(
             k, codes_ref, embed_ref, wro_ref, g2_ref, wcol_ref, qtab, kz, vz, seen, tri, wq2
         )
-        kv_all[my_row, pl.ds(k * PER, PER)] = kv.reshape(PER, rows, 2 * HD)
+        kv_all[slot_of(my_row), pl.ds(k * PER, PER)] = kv.reshape(PER, rows, 2 * HD)
         kv_copy(0, k, my_row, beyond).start()
         kv_copy(1, k, my_row, down).start()
         kv_copy(2, k, my_row, up).start()
-        kv_copy(3, k, my_row, sib).start()
         held[pl.ds(k * tile, tile)] = after
         q2_all[pl.ds(k * PER, PER)] = q2.reshape(PER, rows, 2 * width)
         return carry
@@ -328,13 +354,9 @@
 
     def col_step(j, carry):
         relay(chunks + j)
-        mid = chunks // 2
-        k = jnp.where(j < mid, j, jnp.where(j == mid, chunks - 1, j - 1))
-        for slot in (
-            my_row, beyond, down, turned(beyond, 1), up, turned(beyond, half - 1),
-            far, turned(beyond, 2),
-        ):
-            arrived(k, sibling(slot))
+        k = jnp.where(j < chunks - 2, j, 2 * chunks - 3 - j)
+        for r in (my_row, up, down, far):
+            arrived(k, sibling(r), PAIRED[0])
         col_tile(
             lambda c: q2_all[k * PER + c],
             lambda c: kv_all[:, k * PER + c].reshape(keys, 2 * HD),
@@ -445,8 +467,8 @@
             pltpu.VMEM((tokens, width), F32),
             pltpu.VMEM((col_count, rows, vocab), BF16),
             pltpu.VMEM((2, cols, width), F32),
-            dma((15, chunks)),
-            dma((row_count, chunks)),
+            dma((11, chunks)),
+            dma((row_count + row_count // 2, chunks)),
             dma((col_count,)),
             dma((col_count,)),
             dma((2 * chunks + 6,)),

time: 140 us -> 105 us (0.75)
  the two profiles are of different devices: /device:TPU:3 before, /device:TPU:1 now
where the time goes in v3:
time: 105 us
  Pallas kernels  102 us (97%)
  local copies, waits for them, and re-layouts  2.67 us (3%)
    pallas_call x1, Pallas kernels, front_call(): pl.pallas_call(functools.partial(front_kernel, row_count, col_count), in_...  77.1 us
    pallas_call x1, Pallas kernels, back_call(): pl.pallas_call(functools.partial(back_kernel, col_steps), grid=(col_steps...  24.6 us

profile of v3, /device:TPU:1, one launch (start us, length us, event | category | flops | bytes accessed | tf_op | source)
XLA Modules:
  0.0 104.9 jit_solution(17896057721499994815)
XLA Ops:
  0.6 0.8 dynamic_slice.3
  1.4 0.6 pad_bitcast_fusion.starts_ref
  2.0 1.3 %pad.8.codes_ref = s32[32,128]{1,0:T(8,128)} pad(s32[32,64]{1,0:T(8,128)} %param.15, s32[]{:T(128)} %constant.2.clone.1), padding=0_0x0_64 | pad | bytes 24580 | tf_op jit(solution)/shard_map/jit(_pad)/pad | solution.py:655
  3.3 77.1 %front.1 = (f32[2048,512]{1,0:T(8,128)}, f32[256,512]{1,0:T(8,128)}) custom-call(s32[32,128]{1,0:T(8,128)} %pad.8.codes_ref, s32[1,128]{1,0:T(1,128)} %pad_bitcast_fusion.starts_ref, bf16[512,512]{1,0:T(8,128)(2,1)} %embed_ref.1, f32[1,512]{1,0:T(1,128)} %bitcast.5, bf16[512,1536]{1,0:T(8,128)(2,1)} %wqkv_ref.1, bf16[512,512]{1,0:T(8,128)(2,1)} %wro_ref.1, ...), custom_call_target="tpu_custom_call" | custom-call | tf_op jit(solution)/shard_map/front/pallas_call | solution.py:445
  80.4 24.6 %back.1 = (f32[32,64,512]{2,1,0:T(8,128)}, f32[64,128,128]{2,1,0:T(8,128)}) custom-call(f32[2048,512]{1,0:T(8,128)} %get-tuple-element.4.after_ref, f32[256,512]{1,0:T(8,128)} %get-tuple-element.5.halo_ref, f32[1,512]{1,0:T(1,128)} %bitcast.7, bf16[512,1024]{1,0:T(8,128)(2,1)} %win_ref.1, bf16[1024,512]{1,0:T(8,128)(2,1)} %wout_ref.1, ...), custom_call_target="tpu_custom_call" | custom-call | tf_op jit(solution)/shard_map/back/pallas_call | solution.py:623

commit v4 on v3

--- a/solution.py
+++ b/solution.py
@@ -77,7 +77,8 @@
     rows = codes_ref.shape[0]
     tile = tri.shape[0]
     scale = (HD ** -0.5) * LOG2E
-    rolled = pltpu.roll(codes_ref[...], 128 - PER * k, 1)
+    codes = codes_ref[...]
+    rolled = pltpu.roll(jnp.concatenate([codes, codes], axis=1), 128 - PER * k, 1)
     ids = lax.broadcasted_iota(jnp.int32, (rows, vocab), 1)
     one_hot = jnp.concatenate(
         [jnp.where(rolled[:, c : c + 1] == ids, 1.0, 0.0) for c in range(PER)], axis=0
@@ -124,11 +125,13 @@
     slot, line = place // rows, bias.shape[0] // rows // 2
     key_row = ((slot % line) * 2 + slot // line) * rows + place % rows
     query_row = first + lane - HD
-    seen = (key_row <= query_row) & (key_row >= starts_ref[0:1, :])
+    turn = lax.rem(HD - first + starts_ref.shape[1], starts_ref.shape[1])
+    here = pltpu.roll(jnp.broadcast_to(starts_ref[...], (8, starts_ref.shape[1])), turn, 1)
+    seen = (key_row <= query_row) & (key_row >= here[0:1, :128])
     bias[...] = jnp.where((lane < HD) | seen, 0.0, NEGATIVE).astype(BF16)
 
 
-def col_tile(q_of, kv_of, bias, mixed, rows, keys):
+def col_tile(q_of, kv_of, bias, mixed, at, rows, keys, between):
     low_f = jnp.where(lane_low(keys), 1.0, 0.0)
     low_k = low_f.astype(BF16)
     high_k = (1.0 - low_f).astype(BF16)
@@ -155,19 +158,35 @@
             other = pltpu.roll(jnp.where(low, odd, even), HD, 1)
             num = jnp.where(low, other, keep)
             den = jnp.where(low, keep, other)
-            mixed[c * rows : (c + 1) * rows, p * 128 : p * 128 + 128] = (num / den).astype(BF16)
-
-
-PAIRED = (5, 8, 9, 10)
+            mixed[at, c * rows : (c + 1) * rows, p * 128 : p * 128 + 128] = (num / den).astype(BF16)
+        next(between, None)
+
+
+def feed_forward(mix, before, wco, g3_ref, win, wout, wp, keep):
+    after = before + dot(mix, wco[...])
+    normed = norm_round(after, g3_ref[...])
+    yield
+    inner, quarter = [], win.shape[1] // 4
+    for i in range(4):
+        inner.append(silu(dot(normed, win[:, i * quarter : (i + 1) * quarter])).astype(BF16))
+        yield
+    out = after + dot(jnp.concatenate(inner, axis=1), wout[...])
+    yield
+    keep(out, dot(out.astype(BF16), wp[...]).astype(BF16).astype(F32))
+    yield
+
+
 CORNERS = ((-1, -1), (-1, 1), (1, -1), (1, 1))
 
 
 def front_kernel(
     row_count, col_count,
-    codes_ref, starts_ref, embed_ref, g1_ref, wqkv_ref, wro_ref, g2_ref, wcol_ref, wco_ref,
-    after_ref, halo_ref,
-    qtab, kz, vz, seen, tri, wq2, bias, mixed, kv_all, q2_all, held, hist, edge,
-    kv_send, kv_recv, hist_send, hist_recv, halo_send, halo_recv, out_sem,
+    codes_ref, starts_ref, embed_ref, g1_ref, wqkv_ref, g2_ref, wcol_ref, g3_ref,
+    wro_hbm, wco_hbm, win_hbm, wout_hbm, wp_hbm,
+    bo_ref, co_ref, halo_ref,
+    wro_ref, wco_ref, win_ref, wout_ref, wp_ref,
+    qtab, kz, vz, seen, tri, wq2, bias, mixed, kv_all, q2_all, held, coarse_all, hist, edge,
+    late_sem, kv_send, kv_recv, hist_send, hist_recv, halo_send, halo_recv, out_sem, co_sem,
 ):
     rows = codes_ref.shape[0]
     vocab, width = embed_ref.shape
@@ -192,6 +211,17 @@
     down, up = turned(my_row, 1), turned(my_row, half - 1)
     far = turned(my_row, 2)
 
+    late = [
+        pltpu.make_async_copy(hbm, ref, late_sem.at[i])
+        for i, (hbm, ref) in enumerate(
+            (
+                (wro_hbm, wro_ref), (wco_hbm, wco_ref), (win_hbm, win_ref),
+                (wout_hbm, wout_ref), (wp_hbm, wp_ref),
+            )
+        )
+    ]
+    for copy in late:
+        copy.start()
     halo_ref[...] = jnp.zeros_like(halo_ref)
     def row_by(dr):
         return lax.rem(my_row + dr + row_count, row_count)
@@ -246,63 +276,54 @@
     def slot_of(r):
         return lax.rem(r, 2) * (slots // 2) + lax.div(r, 2)
 
-    def kv_copy(n, k, r, dest):
-        paired = n in PAIRED
-        slot = slot_of(r)
-        if paired:
-            slot = slot - lax.rem(slot, 2)
-        part = kv_all.at[pl.ds(slot, 2 if paired else 1), pl.ds(k * PER, PER)]
-        sem = slots + lax.div(slot, 2) if paired else slot
+    def kv_copy(k, slot, size, stage, dest):
+        part = kv_all.at[pl.ds(slot, size), pl.ds(k * PER, PER)]
         return pltpu.make_async_remote_copy(
             src_ref=part, dst_ref=part,
-            send_sem=kv_send.at[n, k], recv_sem=kv_recv.at[sem, k],
+            send_sem=kv_send.at[k], recv_sem=kv_recv.at[stage, k],
             device_id={"row": dest}, device_id_type=MESH,
         )
 
-    def arrived(k, r, n=0):
-        kv_copy(n, k, r, sib).wait_recv()
-
-    up_beyond, down_beyond, far_beyond = across(up), across(down), across(far)
+    def send(k, r, stage, dest):
+        kv_copy(k, slot_of(r), 1, stage, dest).start()
+
+    def arrived(k, stage, size):
+        kv_copy(k, 0, size, stage, sib).wait_recv()
 
     def relay(s):
         k1 = s - 2
 
         @pl.when((k1 >= 0) & (k1 < chunks))
         def _():
-            arrived(k1, beyond)
-            kv_copy(3, k1, beyond, down).start()
-            kv_copy(4, k1, beyond, up).start()
-            kv_copy(5, k1, my_row, sib).start()
-            arrived(k1, up)
-            arrived(k1, down)
+            arrived(k1, 0, 3)
+            send(k1, beyond, 1, down)
+            send(k1, beyond, 1, up)
             even = lax.rem(k1, 2) == 0
 
             @pl.when(even)
             def _():
-                kv_copy(6, k1, up, down).start()
+                send(k1, up, 1, down)
 
             @pl.when(jnp.logical_not(even))
             def _():
-                kv_copy(6, k1, down, up).start()
-
-        mid = chunks // 2
-        k2 = jnp.where(s < mid + 4, s - 3, s - 4)
-
-        @pl.when((k2 >= 0) & (k2 < chunks) & (s != mid + 4))
-        def _():
-            arrived(k2, far)
-            kv_copy(7, k2, far, beyond).start()
-            arrived(k2, up_beyond)
-            kv_copy(8, k2, up, sib).start()
-            arrived(k2, down_beyond)
-            kv_copy(9, k2, down, sib).start()
-
-        k3 = s - 5
+                send(k1, down, 1, up)
+
+        k2 = s - 4
+
+        @pl.when((k2 >= 0) & (k2 < chunks))
+        def _():
+            arrived(k2, 1, 3)
+            send(k2, far, 2, beyond)
+
+        k3 = s - 6
 
         @pl.when((k3 >= 0) & (k3 < chunks))
         def _():
-            arrived(k3, far_beyond)
-            kv_copy(10, k3, far, sib).start()
+            arrived(k3, 2, 1)
+            line = lax.rem(my_row, 2) * (slots // 2)
+            kv_copy(k3, line, slots // 2, 3, sib).start()
+
+    late[0].wait()
 
     def row_step(k, carry):
         relay(k)
@@ -310,10 +331,10 @@
             k, codes_ref, embed_ref, wro_ref, g2_ref, wcol_ref, qtab, kz, vz, seen, tri, wq2
         )
         kv_all[slot_of(my_row), pl.ds(k * PER, PER)] = kv.reshape(PER, rows, 2 * HD)
-        kv_copy(0, k, my_row, beyond).start()
-        kv_copy(1, k, my_row, down).start()
-        kv_copy(2, k, my_row, up).start()
-        held[pl.ds(k * tile, tile)] = after
+        send(k, my_row, 0, beyond)
+        send(k, my_row, 0, down)
+        send(k, my_row, 0, up)
+        held[k] = after.reshape(rows, PER, width)
         q2_all[pl.ds(k * PER, PER)] = q2.reshape(PER, rows, 2 * width)
         return carry
 
@@ -338,7 +359,7 @@
     def side_copy(which, dc):
         c = 0 if which == 0 else cols - 1
         at = left_at + rows if which == 0 else left_at
-        return halo_copy(side_sem + which, held.at[pl.ds(c * rows, rows)], at, rows, 0, dc)
+        return halo_copy(side_sem + which, coarse_all.at[pl.ds(c * rows, rows)], at, rows, 0, dc)
 
     def corner_copy(i, dr, dc):
         k = 0 if dc < 0 else chunks - 1
@@ -347,61 +368,92 @@
             side_sem + 2 + i, edge.at[0 if dr < 0 else 1, pl.ds(k * PER, PER)], at, PER, dr, dc
         )
 
-    def out_copy(k):
-        return pltpu.make_async_copy(
-            held.at[pl.ds(k * tile, tile)], after_ref.at[pl.ds(k * tile, tile)], out_sem.at[k]
-        )
-
-    def col_step(j, carry):
+    def out_copies(k):
+        part = pl.ds(k * tile, tile)
+        return (
+            pltpu.make_async_copy(
+                held.at[k], bo_ref.at[pl.ds(0, rows), pl.ds(k * PER, PER)], out_sem.at[k]
+            ),
+            pltpu.make_async_copy(coarse_all.at[part], co_ref.at[part], co_sem.at[k]),
+        )
+
+    def chunk_of(j):
+        return jnp.where(j < chunks - 2, j, 2 * chunks - 3 - j)
+
+    def feed(j):
+        k = chunk_of(j)
+
+        def keep(out, coarse):
+            held[k] = jnp.swapaxes(out.reshape(PER, rows, width), 0, 1)
+            coarse_all[pl.ds(k * tile, tile)] = coarse
+            grid = coarse.reshape(PER, rows, coarse.shape[1])
+            edge[0, pl.ds(k * PER, PER)] = grid[:, 0]
+            edge[1, pl.ds(k * PER, PER)] = grid[:, rows - 1]
+
+        return feed_forward(
+            mixed[lax.rem(j, 2)], held[k].reshape(tile, width), wco_ref, g3_ref, win_ref,
+            wout_ref, wp_ref, keep,
+        )
+
+    def pass_on(j):
+        k = chunk_of(j)
+        for copy in out_copies(k):
+            copy.start()
+
+        @pl.when(there(-1, 0))
+        def _():
+            edge_copy(0, k, -1).start()
+
+        @pl.when(there(1, 0))
+        def _():
+            edge_copy(1, k, 1).start()
+
+        for which, dc in ((0, -1), (1, 1)):
+            last = 0 if which == 0 else chunks - 1
+
+            @pl.when(there(0, dc) & (k == last))
+            def _():
+                side_copy(which, dc).start()
+
+        for i, (dr, dc) in enumerate(CORNERS):
+            last = 0 if dc < 0 else chunks - 1
+
+            @pl.when(there(dr, dc) & (k == last))
+            def _():
+                corner_copy(i, dr, dc).start()
+
+    def attend(j, between):
         relay(chunks + j)
-        k = jnp.where(j < chunks - 2, j, 2 * chunks - 3 - j)
-        for r in (my_row, up, down, far):
-            arrived(k, sibling(r), PAIRED[0])
+        k = chunk_of(j)
+        arrived(k, 3, slots // 2)
         col_tile(
             lambda c: q2_all[k * PER + c],
             lambda c: kv_all[:, k * PER + c].reshape(keys, 2 * HD),
-            bias, mixed, rows, keys,
-        )
-        after = held[pl.ds(k * tile, tile)] + dot(mixed[...], wco_ref[...])
-        held[pl.ds(k * tile, tile)] = after
-        out_copy(k).start()
-        grid = after.reshape(PER, rows, width)
-        edge[0, pl.ds(k * PER, PER)] = grid[:, 0]
-        edge[1, pl.ds(k * PER, PER)] = grid[:, rows - 1]
-
-        @pl.when(there(-1, 0))
-        def _():
-            edge_copy(0, k, -1).start()
-
-        @pl.when(there(1, 0))
-        def _():
-            edge_copy(1, k, 1).start()
-
-        for which, dc in ((0, -1), (1, 1)):
-            last = 0 if which == 0 else chunks - 1
-
-            @pl.when(there(0, dc) & (k == last))
-            def _():
-                side_copy(which, dc).start()
-
-        for i, (dr, dc) in enumerate(CORNERS):
-            last = 0 if dc < 0 else chunks - 1
-
-            @pl.when(there(dr, dc) & (k == last))
-            def _():
-                corner_copy(i, dr, dc).start()
-
+            bias, mixed, lax.rem(j, 2), rows, keys, between,
+        )
+        for _ in between:
+            pass
+
+    def col_step(j, carry):
+        attend(j, feed(j - 1))
+        pass_on(j - 1)
         return carry
 
-    lax.fori_loop(0, chunks, col_step, 0)
+    attend(0, iter(()))
+    for copy in late[1:]:
+        copy.wait()
+    lax.fori_loop(1, chunks, col_step, 0)
+    for _ in feed(chunks - 1):
+        pass
+    pass_on(chunks - 1)
 
     for d in range(1, col_count):
         hist_copy(d, my_col).wait_send()
 
     def finish(k, carry):
-        for n in range(kv_send.shape[0]):
-            kv_copy(n, k, my_row, sib).wait_send()
-        out_copy(k).wait()
+        kv_copy(k, 0, 7 + slots // 2, 0, sib).wait_send()
+        for copy in out_copies(k):
+            copy.wait()
 
         @pl.when(there(-1, 0))
         def _():
@@ -432,28 +484,30 @@
     return pl.BlockSpec(shape, lambda *_: (0,) * len(shape))
 
 
-def front_call(codes, starts, embed, g1, wqkv, wro, g2, wcol, wco, cols):
+def front_call(codes, starts, embed, g1, wqkv, g2, wcol, g3, wro, wco, win, wout, wp):
     vocab, width = embed.shape
-    rows = codes.shape[0]
+    rows, cols = codes.shape
+    ch = wp.shape[1]
     row_count, col_count = lax.axis_size("row"), lax.axis_size("col")
     tokens = rows * cols
     tile = rows * PER
     chunks = cols // PER
-    halo = -(-(2 * cols + 2 * rows + 4 * PER) // tile) * tile
+    halo = 2 * cols + 2 * rows + 4 * PER
     dma = pltpu.SemaphoreType.DMA
-    args = (codes, starts, embed, g1, wqkv, wro, g2, wcol, wco)
+    early = (codes, starts, embed, g1, wqkv, g2, wcol, g3)
+    late = (wro, wco, win, wout, wp)
+    anywhere, vmem = pl.BlockSpec(memory_space=pl.ANY), pl.BlockSpec(memory_space=pltpu.VMEM)
     return pl.pallas_call(
         functools.partial(front_kernel, row_count, col_count),
-        in_specs=[pl.BlockSpec(memory_space=pltpu.VMEM)] * len(args),
-        out_specs=[
-            pl.BlockSpec(memory_space=pl.ANY),
-            pl.BlockSpec(memory_space=pltpu.VMEM),
+        in_specs=[vmem] * len(early) + [anywhere] * len(late),
+        out_specs=[anywhere, anywhere, vmem],
+        out_shape=[
+            jax.ShapeDtypeStruct((rows, cols, width), F32),
+            jax.ShapeDtypeStruct((tokens, ch), F32),
+            jax.ShapeDtypeStruct((halo, ch), F32),
         ],
-        out_shape=[
-            jax.ShapeDtypeStruct((tokens, width), F32),
-            jax.ShapeDtypeStruct((halo, width), F32),
-        ],
-        scratch_shapes=[
+        scratch_shapes=[pltpu.VMEM(x.shape, x.dtype) for x in late]
+        + [
             pltpu.VMEM((vocab, width), BF16),
             pltpu.VMEM((HEADS, vocab, 128), BF16),
             pltpu.VMEM((HEADS, vocab, 128), BF16),
@@ -461,33 +515,31 @@
             pltpu.VMEM((tile, tile), BF16),
             pltpu.VMEM((width, 2 * width), BF16),
             pltpu.VMEM((row_count * rows, 128), BF16),
-            pltpu.VMEM((tile, width), BF16),
+            pltpu.VMEM((2, tile, width), BF16),
             pltpu.VMEM((row_count, cols, rows, 2 * HD), BF16),
             pltpu.VMEM((cols, rows, 2 * width), BF16),
-            pltpu.VMEM((tokens, width), F32),
+            pltpu.VMEM((chunks, rows, PER, width), F32),
+            pltpu.VMEM((tokens, ch), F32),
             pltpu.VMEM((col_count, rows, vocab), BF16),
-            pltpu.VMEM((2, cols, width), F32),
-            dma((11, chunks)),
-            dma((row_count + row_count // 2, chunks)),
+            pltpu.VMEM((2, cols, ch), F32),
+            dma((len(late),)),
+            dma((chunks,)),
+            dma((4, chunks)),
             dma((col_count,)),
             dma((col_count,)),
             dma((2 * chunks + 6,)),
             dma((2 * chunks + 6,)),
+            dma((chunks,)),
             dma((chunks,)),
         ],
         compiler_params=pltpu.CompilerParams(
             vmem_limit_bytes=VMEM_LIMIT, collective_id=0, has_side_effects=True
         ),
         name="front",
-    )(*args)
-
-
-def back_kernel(
-    col_steps,
-    after_ref, halo_ref, g3_ref, win_ref, wout_ref, wp_ref, k1_ref, k2_ref,
-    bo_ref, img_ref,
-    ext, w1, w2, cat, fine,
-):
+    )(*early, *late)
+
+
+def back_kernel(bo_in, co_ref, halo_ref, k1_ref, k2_ref, bo_ref, img_ref, ext, w1, w2, cat, fine, hold, in_sem, out_sem):
     k = pl.program_id(0)
     erows, ring, ch = ext.shape
     rows = erows - 2
@@ -497,28 +549,25 @@
     my_row, my_col = lax.axis_index("row"), lax.axis_index("col")
     at_top, at_bottom = my_row == 0, my_row == lax.axis_size("row") - 1
     at_left, at_right = my_col == 0, my_col == lax.axis_size("col") - 1
-
-    def cells(after):
-        normed = norm_round(after, g3_ref[...])
-        inner = silu(dot(normed, win_ref[...])).astype(BF16)
-        out = after + dot(inner, wout_ref[...])
-        coarse = dot(out.astype(BF16), wp_ref[...]).astype(BF16).astype(F32)
-        return out, coarse
+    per = rows // in_sem.shape[0]
+
+    def taken(i):
+        part = pl.ds(i * per, per)
+        return pltpu.make_async_copy(bo_in.at[part], hold.at[part], in_sem.at[i])
+
+    def given(i):
+        part = pl.ds(i * per, per)
+        return pltpu.make_async_copy(hold.at[part], bo_ref.at[part], out_sem.at[i])
 
     @pl.when(k == 0)
     def _():
+        for i in range(in_sem.shape[0]):
+            taken(i).start()
         ext[...] = jnp.zeros_like(ext)
-
-    @pl.when(k < col_steps)
-    def _():
-        out, coarse = cells(after_ref[...])
-        bo_ref[...] = jnp.swapaxes(out.reshape(PER, rows, out.shape[1]), 0, 1)
-        at = pl.multiple_of(k * PER, PER)
-        ext[1 : rows + 1, pl.ds(at, PER), :] = jnp.swapaxes(coarse.reshape(PER, rows, ch), 0, 1)
-
-    @pl.when(k == col_steps)
-    def _():
-        _, coarse = cells(halo_ref[...])
+        for c in range(0, cols, PER):
+            part = co_ref[c * rows : (c + PER) * rows].reshape(PER, rows, ch)
+            ext[1 : rows + 1, c : c + PER, :] = jnp.swapaxes(part, 0, 1)
+        coarse = halo_ref[...]
         zero = jnp.float32(0.0)
         ext[0, 0:cols] = jnp.where(at_top, zero, coarse[0:cols])
         ext[rows + 1, 0:cols] = jnp.where(at_bottom, zero, coarse[cols : 2 * cols])
@@ -567,7 +616,7 @@
         col_keep = jnp.where(
             ((place == ring - 1) & at_left) | ((place == cols) & at_right), 0.0, 1.0
         )
-        group = 3
+        group = 11
 
         def first_conv(g, carry):
             e0 = g * group
@@ -593,9 +642,8 @@
 
         lax.fori_loop(0, pairs // group, first_conv, 0)
 
-    @pl.when(k > col_steps)
-    def _():
-        m = k - col_steps - 1
+    if True:
+        m = k
         y0 = m * fine_step
         left = jnp.concatenate(
             [
@@ -611,28 +659,28 @@
                 img_ref[i, pl.ds(b, cols, stride=2), :] = (
                     second[i * cols : (i + 1) * cols, b * ch : (b + 1) * ch] + up
                 )
-
-
-def back_call(after, halo, g3, win, wout, wp, k1, k2, rows, cols):
-    width = after.shape[1]
-    ch = wp.shape[1]
-    tile = rows * PER
-    col_steps = cols // PER
+    taken(k).wait()
+    given(k).start()
+
+    @pl.when(k == pl.num_programs(0) - 1)
+    def _():
+        for i in range(in_sem.shape[0]):
+            given(i).wait()
+
+
+def back_call(block_out, coarse, halo, k1, k2):
+    rows, cols, _ = block_out.shape
+    ch = coarse.shape[1]
     ring = cols + 16
-    fine_step = 8
+    fine_step = 16
+    anywhere = pl.BlockSpec(memory_space=pl.ANY)
     return pl.pallas_call(
-        functools.partial(back_kernel, col_steps),
-        grid=(col_steps + 1 + 2 * rows // fine_step,),
-        in_specs=[pl.BlockSpec((tile, width), lambda i: (jnp.minimum(i, col_steps - 1), 0))]
-        + [full(x.shape) for x in (halo, g3, win, wout, wp, k1, k2)],
-        out_specs=[
-            pl.BlockSpec((rows, PER, width), lambda i: (0, jnp.minimum(i, col_steps - 1), 0)),
-            pl.BlockSpec(
-                (fine_step, 2 * cols, ch), lambda i: (jnp.maximum(i - col_steps - 1, 0), 0, 0)
-            ),
-        ],
+        back_kernel,
+        grid=(2 * rows // fine_step,),
+        in_specs=[anywhere] + [full(x.shape) for x in (coarse, halo, k1, k2)],
+        out_specs=[anywhere, pl.BlockSpec((fine_step, 2 * cols, ch), lambda i: (i, 0, 0))],
         out_shape=[
-            jax.ShapeDtypeStruct((rows, cols, width), F32),
+            jax.ShapeDtypeStruct(block_out.shape, F32),
             jax.ShapeDtypeStruct((2 * rows, 2 * cols, ch), F32),
         ],
         scratch_shapes=[
@@ -641,30 +689,24 @@
             pltpu.VMEM((12 * ch, 2 * ch), BF16),
             pltpu.VMEM((rows + 2, ring, 3 * ch), BF16),
             pltpu.VMEM((2 * rows + 2, ring, 4 * ch), BF16),
+            pltpu.VMEM(block_out.shape, F32),
+            pltpu.SemaphoreType.DMA((2 * rows // fine_step,)),
+            pltpu.SemaphoreType.DMA((2 * rows // fine_step,)),
         ],
         compiler_params=pltpu.CompilerParams(vmem_limit_bytes=VMEM_LIMIT),
         name="back",
-    )(after, halo, g3, win, wout, wp, k1, k2)
+    )(block_out, coarse, halo, k1, k2)
 
 
 def per_device(
     codes, starts, embed, gain_one, row_qkv, row_out, gain_two, col_qkv, col_out,
     gain_three, mlp_in, mlp_out, project, conv_one, conv_two,
 ):
-    rows, cols = codes.shape
-    wide = jnp.pad(codes, ((0, 0), (0, 128 - cols)))
-    my_starts = lax.dynamic_slice_in_dim(starts, lax.axis_index("row") * rows, rows)
-    my_starts = jnp.pad(my_starts, (HD, 128 - HD - rows))[None]
-    after_col, halo = front_call(
-        wide, my_starts, embed, gain_one[None], row_qkv, row_out, gain_two[None],
-        col_qkv, col_out, cols,
+    block_out, coarse, halo = front_call(
+        codes, starts[None], embed, gain_one[None], row_qkv, gain_two[None], col_qkv,
+        gain_three[None], row_out, col_out, mlp_in, mlp_out, project,
     )
-    return tuple(
-        back_call(
-            after_col, halo, gain_three[None], mlp_in, mlp_out, project, conv_one, conv_two,
-            rows, cols,
-        )
-    )
+    return tuple(back_call(block_out, coarse, halo, conv_one, conv_two))
 
 
 def solution(mesh):

time: 105 us -> 84.6 us (0.81)
  the two profiles are of different devices: /device:TPU:1 before, /device:TPU:3 now
where the time goes in v4:
time: 84.6 us; the launch traced here: 83.7 us
  Pallas kernels  83.1 us (98%)
    pallas_call x1, Pallas kernels, front_call(): pl.pallas_call(functools.partial(front_kernel, row_count, col_count), in_...  70.5 us
    pallas_call x1, Pallas kernels, back_call(): pl.pallas_call(back_kernel, grid=(2 * rows // fine_step,), in_specs=[anyw...  12.6 us

profile of v4, /device:TPU:3, one launch (start us, length us, event | category | flops | bytes accessed | tf_op | source)
XLA Modules:
  0.0 83.7 jit_solution(5940918072161765029)
XLA Ops:
  0.6 70.5 %front.1 = (f32[32,64,512]{2,1,0:T(8,128)}, f32[2048,128]{1,0:T(8,128)}, f32[224,128]{1,0:T(8,128)}) custom-call(s32[32,64]{1,0:T(8,128)} %codes_ref.1, s32[1,512]{1,0:T(1,128)} %bitcast.4, bf16[512,512]{1,0:T(8,128)(2,1)} %embed_ref.1, f32[1,512]{1,0:T(1,128)} %bitcast.5, bf16[512,1536]{1,0:T(8,128)(2,1)} %wqkv_ref.1, f32[1,512]{1,0:T(1,128)} %bitcast.6, ...), custom_call_target="tpu_custom_call" | custom-call | tf_op jit(solution)/shard_map/front/pallas_call | solution.py:500
  71.2 12.6 %back.1 = (f32[32,64,512]{2,1,0:T(8,128)}, f32[64,128,128]{2,1,0:T(8,128)}) custom-call(f32[32,64,512]{2,1,0:T(8,128)} %get-tuple-element.5.bo_in, f32[2048,128]{1,0:T(8,128)} %get-tuple-element.6.co_ref, f32[224,128]{1,0:T(8,128)} %get-tuple-element.7.halo_ref, bf16[3,3,128,128]{3,2,1,0:T(8,128)(2,1)} %k1_ref.1, bf16[3,3,128,128]{3,2,1,0:T(8,128)(2,1)} %k2_ref.1), custom_call_target="tpu_custom_call" | custom-call | tf_op jit(solution)/shard_map/back/pallas_call | solution.py:677

commit v5 on v4

--- a/solution.py
+++ b/solution.py
@@ -32,7 +32,8 @@
 
 
 def silu(v):
-    return v / (1.0 + jnp.exp(-v))
+    h = 0.5 * v
+    return h + h * jnp.tanh(h)
 
 
 def lane_low(rows):
@@ -43,7 +44,7 @@
 AHEAD = 2
 
 
-def row_setup(embed_ref, g1_ref, wqkv_ref, wcol_ref, qtab, kz, vz, tri, wq2, rows):
+def row_setup(embed_ref, g1_ref, wqkv_ref, qtab, kz, vz, tri, rows):
     vocab, width = embed_ref.shape
     tile = tri.shape[0]
     scale = (HD ** -0.5) * LOG2E
@@ -63,16 +64,9 @@
     tri[...] = jnp.where(
         (out_t % rows == in_t % rows) & (in_t // rows <= out_t // rows), 1.0, 0.0
     ).astype(BF16)
-    lowd = lane_low(width)
-    for p in range(HEADS // 2):
-        w = wcol_ref[:, p * 128 : p * 128 + 128].astype(F32)
-        wq2[:, (2 * p) * 128 : (2 * p + 1) * 128] = jnp.where(lowd, w, 0.0).astype(BF16)
-        wq2[:, (2 * p + 1) * 128 : (2 * p + 2) * 128] = jnp.where(
-            lowd, pltpu.roll(w, HD, 1), 0.0
-        ).astype(BF16)
-
-
-def row_tile(k, codes_ref, embed_ref, wro_ref, g2_ref, wcol_ref, qtab, kz, vz, seen, tri, wq2):
+
+
+def row_tile(k, codes_ref, embed_ref, wro_ref, g2_ref, wcol_ref, qtab, kz, vz, seen, tri):
     vocab, width = embed_ref.shape
     rows = codes_ref.shape[0]
     tile = tri.shape[0]
@@ -109,14 +103,16 @@
             outs = []
     after = emb + dot(jnp.concatenate(mixed, axis=1), wro_ref[...])
     normed = norm_round(after, g2_ref[...])
-    q2 = dot(normed, wq2[...]) * scale
+    proj = dot(normed, wcol_ref[...])
     lane = lax.broadcasted_iota(jnp.int32, (tile, 128), 1)
     row = lax.broadcasted_iota(jnp.int32, (tile, 128), 0) % rows
     mark = jnp.where(lane == HD + row, 1.0, 0.0)
-    q2 = jnp.concatenate(
-        [(q2[:, h * 128 : h * 128 + 128] + mark).astype(BF16) for h in range(HEADS)], axis=1
-    )
-    return after, q2, dot(normed, wcol_ref[:, width:]).astype(BF16)
+    q2 = []
+    for p in range(HEADS // 2):
+        pair = proj[:, p * 128 : p * 128 + 128] * scale
+        q2.append(jnp.where(low, pair, mark).astype(BF16))
+        q2.append(jnp.where(low, pltpu.roll(pair, HD, 1), mark).astype(BF16))
+    return after, jnp.concatenate(q2, axis=1), proj[:, width:].astype(BF16)
 
 
 def set_bias(bias, starts_ref, first, rows):
@@ -181,15 +177,15 @@
 
 def front_kernel(
     row_count, col_count,
-    codes_ref, starts_ref, embed_ref, g1_ref, wqkv_ref, g2_ref, wcol_ref, g3_ref,
-    wro_hbm, wco_hbm, win_hbm, wout_hbm, wp_hbm,
+    codes_ref, starts_ref, g1_ref, g2_ref, g3_ref,
+    embed_hbm, wqkv_hbm, wcol_hbm, wro_hbm, wco_hbm, win_hbm, wout_hbm, wp_hbm,
     bo_ref, co_ref, halo_ref,
-    wro_ref, wco_ref, win_ref, wout_ref, wp_ref,
-    qtab, kz, vz, seen, tri, wq2, bias, mixed, kv_all, q2_all, held, coarse_all, hist, edge,
+    embed_ref, wqkv_ref, wcol_ref, wro_ref, wco_ref, win_ref, wout_ref, wp_ref,
+    qtab, kz, vz, seen, tri, bias, mixed, kv_all, q2_all, held, coarse_all, hist, edge,
     late_sem, kv_send, kv_recv, hist_send, hist_recv, halo_send, halo_recv, out_sem, co_sem,
 ):
     rows = codes_ref.shape[0]
-    vocab, width = embed_ref.shape
+    vocab, width = embed_hbm.shape
     slots, cols = kv_all.shape[0], kv_all.shape[1]
     keys = slots * rows
     tile = PER * rows
@@ -211,18 +207,8 @@
     down, up = turned(my_row, 1), turned(my_row, half - 1)
     far = turned(my_row, 2)
 
-    late = [
-        pltpu.make_async_copy(hbm, ref, late_sem.at[i])
-        for i, (hbm, ref) in enumerate(
-            (
-                (wro_hbm, wro_ref), (wco_hbm, wco_ref), (win_hbm, win_ref),
-                (wout_hbm, wout_ref), (wp_hbm, wp_ref),
-            )
-        )
-    ]
-    for copy in late:
-        copy.start()
     halo_ref[...] = jnp.zeros_like(halo_ref)
+    hist[...] = jnp.zeros_like(hist)
     def row_by(dr):
         return lax.rem(my_row + dr + row_count, row_count)
 
@@ -244,6 +230,19 @@
                 ok = t if ok is None else ok & t
         return ok
 
+    late = [
+        pltpu.make_async_copy(hbm, ref, late_sem.at[i])
+        for i, (hbm, ref) in enumerate(
+            (
+                (embed_hbm, embed_ref), (wqkv_hbm, wqkv_ref), (wcol_hbm, wcol_ref),
+                (wro_hbm, wro_ref), (wco_hbm, wco_ref), (win_hbm, win_ref),
+                (wout_hbm, wout_ref), (wp_hbm, wp_ref),
+            )
+        )
+    ]
+    for copy in late:
+        copy.start()
+
     ids = lax.broadcasted_iota(jnp.int32, (rows, vocab), 1)
     codes = codes_ref[...]
     own = jnp.zeros((rows, vocab), F32)
@@ -261,16 +260,21 @@
         )
 
     for d in range(1, col_count):
-        hist_copy(d, my_col).start()
-
-    row_setup(embed_ref, g1_ref, wqkv_ref, wcol_ref, qtab, kz, vz, tri, wq2, rows)
-    set_bias(bias, starts_ref, my_row * rows, rows)
+        @pl.when(my_col + d < col_count)
+        def _():
+            hist_copy(d, my_col).start()
+
+    for copy in late[:2]:
+        copy.wait()
+    row_setup(embed_ref, g1_ref, wqkv_ref, qtab, kz, vz, tri, rows)
 
     for d in range(1, col_count):
-        hist_copy(d, lax.rem(my_col + d, col_count)).wait_recv()
+        @pl.when(my_col >= d)
+        def _():
+            hist_copy(d, lax.rem(my_col - d + col_count, col_count)).wait_recv()
     base = jnp.zeros((rows, vocab), F32)
     for c in range(col_count):
-        base = base + jnp.where(c < my_col, 1.0, 0.0) * hist[c].astype(F32)
+        base = base + jnp.where(c < my_col, hist[c].astype(F32), 0.0)
     seen[...] = base
 
     def slot_of(r):
@@ -291,7 +295,7 @@
         kv_copy(k, 0, size, stage, sib).wait_recv()
 
     def relay(s):
-        k1 = s - 2
+        k1 = s - 3
 
         @pl.when((k1 >= 0) & (k1 < chunks))
         def _():
@@ -308,14 +312,14 @@
             def _():
                 send(k1, down, 1, up)
 
-        k2 = s - 4
+        k2 = s - 5
 
         @pl.when((k2 >= 0) & (k2 < chunks))
         def _():
             arrived(k2, 1, 3)
             send(k2, far, 2, beyond)
 
-        k3 = s - 6
+        k3 = s - 7
 
         @pl.when((k3 >= 0) & (k3 < chunks))
         def _():
@@ -323,12 +327,13 @@
             line = lax.rem(my_row, 2) * (slots // 2)
             kv_copy(k3, line, slots // 2, 3, sib).start()
 
-    late[0].wait()
+    for copy in late[2:4]:
+        copy.wait()
 
     def row_step(k, carry):
         relay(k)
         after, q2, kv = row_tile(
-            k, codes_ref, embed_ref, wro_ref, g2_ref, wcol_ref, qtab, kz, vz, seen, tri, wq2
+            k, codes_ref, embed_ref, wro_ref, g2_ref, wcol_ref, qtab, kz, vz, seen, tri
         )
         kv_all[slot_of(my_row), pl.ds(k * PER, PER)] = kv.reshape(PER, rows, 2 * HD)
         send(k, my_row, 0, beyond)
@@ -378,7 +383,7 @@
         )
 
     def chunk_of(j):
-        return jnp.where(j < chunks - 2, j, 2 * chunks - 3 - j)
+        return j
 
     def feed(j):
         k = chunk_of(j)
@@ -439,8 +444,9 @@
         pass_on(j - 1)
         return carry
 
+    set_bias(bias, starts_ref, my_row * rows, rows)
     attend(0, iter(()))
-    for copy in late[1:]:
+    for copy in late[4:]:
         copy.wait()
     lax.fori_loop(1, chunks, col_step, 0)
     for _ in feed(chunks - 1):
@@ -448,7 +454,9 @@
     pass_on(chunks - 1)
 
     for d in range(1, col_count):
-        hist_copy(d, my_col).wait_send()
+        @pl.when(my_col + d < col_count)
+        def _():
+            hist_copy(d, my_col).wait_send()
 
     def finish(k, carry):
         kv_copy(k, 0, 7 + slots // 2, 0, sib).wait_send()
@@ -494,8 +502,8 @@
     chunks = cols // PER
     halo = 2 * cols + 2 * rows + 4 * PER
     dma = pltpu.SemaphoreType.DMA
-    early = (codes, starts, embed, g1, wqkv, g2, wcol, g3)
-    late = (wro, wco, win, wout, wp)
+    early = (codes, starts, g1, g2, g3)
+    late = (embed, wqkv, wcol, wro, wco, win, wout, wp)
     anywhere, vmem = pl.BlockSpec(memory_space=pl.ANY), pl.BlockSpec(memory_space=pltpu.VMEM)
     return pl.pallas_call(
         functools.partial(front_kernel, row_count, col_count),
@@ -513,7 +521,6 @@
             pltpu.VMEM((HEADS, vocab, 128), BF16),
             pltpu.VMEM((rows, vocab), F32),
             pltpu.VMEM((tile, tile), BF16),
-            pltpu.VMEM((width, 2 * width), BF16),
             pltpu.VMEM((row_count * rows, 128), BF16),
             pltpu.VMEM((2, tile, width), BF16),
             pltpu.VMEM((row_count, cols, rows, 2 * HD), BF16),

time: 84.6 us -> 80.4 us (0.950)
  Pallas kernels: 83.1 us -> 79.5 us
    pallas_call x1, Pallas kernels: 70.5 us -> 67.1 us  [front_call(): pl.pallas_call(functools.partial(front_kernel, row_count, col_count), in_...]
where the time goes in v5:
time: 80.4 us; the launch traced here: 80.2 us
  Pallas kernels  79.5 us (99%)
    pallas_call x1, Pallas kernels, front_call(): pl.pallas_call(functools.partial(front_kernel, row_count, col_count), in_...  67.1 us
    pallas_call x1, Pallas kernels, back_call(): pl.pallas_call(back_kernel, grid=(2 * rows // fine_step,), in_specs=[anyw...  12.4 us

profile of v5, /device:TPU:3, one launch (start us, length us, event | category | flops | bytes accessed | tf_op | source)
XLA Modules:
  0.0 80.2 jit_solution(9612817887770957231)
XLA Ops:
  0.6 67.1 %front.1 = (f32[32,64,512]{2,1,0:T(8,128)}, f32[2048,128]{1,0:T(8,128)}, f32[224,128]{1,0:T(8,128)}) custom-call(s32[32,64]{1,0:T(8,128)} %codes_ref.1, s32[1,512]{1,0:T(1,128)} %bitcast.4, f32[1,512]{1,0:T(1,128)} %bitcast.5, f32[1,512]{1,0:T(1,128)} %bitcast.6, f32[1,512]{1,0:T(1,128)} %bitcast.7, bf16[512,512]{1,0:T(8,128)(2,1)} %embed_hbm.1, ...), custom_call_target="tpu_custom_call" | custom-call | tf_op jit(solution)/shard_map/front/pallas_call | solution.py:508
  67.8 12.4 %back.1 = (f32[32,64,512]{2,1,0:T(8,128)}, f32[64,128,128]{2,1,0:T(8,128)}) custom-call(f32[32,64,512]{2,1,0:T(8,128)} %get-tuple-element.5.bo_in, f32[2048,128]{1,0:T(8,128)} %get-tuple-element.6.co_ref, f32[224,128]{1,0:T(8,128)} %get-tuple-element.7.halo_ref, bf16[3,3,128,128]{3,2,1,0:T(8,128)(2,1)} %k1_ref.1, bf16[3,3,128,128]{3,2,1,0:T(8,128)(2,1)} %k2_ref.1), custom_call_target="tpu_custom_call" | custom-call | tf_op jit(solution)/shard_map/back/pallas_call | solution.py:684

commit v6 on v5

--- a/solution.py
+++ b/solution.py
@@ -625,8 +625,7 @@
         )
         group = 11
 
-        def first_conv(g, carry):
-            e0 = g * group
+        def first_sums(e0):
             left = jnp.concatenate(
                 [
                     jnp.concatenate([cat[e0 + i], cat[e0 + i + 1]], axis=1)
@@ -634,7 +633,10 @@
                 ],
                 axis=0,
             )
-            y = silu(dot(left, w1[...]))
+            return dot(left, w1[...])
+
+        def first_keep(e0, sums):
+            y = silu(sums)
             for i in range(group):
                 for half in range(2):
                     f = 2 * (e0 + i) + half
@@ -645,9 +647,13 @@
                     fine[f] = jnp.concatenate(
                         [pltpu.roll(f1, 1, 0), f0, f1, pltpu.roll(f0, ring - 1, 0)], axis=1
                     ).astype(BF16)
-            return carry
-
-        lax.fori_loop(0, pairs // group, first_conv, 0)
+
+        nxt = first_sums(0)
+        for e0 in range(0, pairs, group):
+            sums = nxt
+            if e0 + group < pairs:
+                nxt = first_sums(e0 + group)
+            first_keep(e0, sums)
 
     if True:
         m = k

time: 80.4 us -> 79.8 us (level)
  no operation moved by 1% of the time
where the time goes in v6:
time: 79.8 us; the launch traced here: 79.6 us
  Pallas kernels  78.9 us (99%)
    pallas_call x1, Pallas kernels, front_call(): pl.pallas_call(functools.partial(front_kernel, row_count, col_count), in_...  67.1 us
    pallas_call x1, Pallas kernels, back_call(): pl.pallas_call(back_kernel, grid=(2 * rows // fine_step,), in_specs=[anyw...  11.8 us

profile of v6, /device:TPU:3, one launch (start us, length us, event | category | flops | bytes accessed | tf_op | source)
XLA Modules:
  0.0 79.6 jit_solution(16923020587916970792)
XLA Ops:
  0.6 67.1 %front.1 = (f32[32,64,512]{2,1,0:T(8,128)}, f32[2048,128]{1,0:T(8,128)}, f32[224,128]{1,0:T(8,128)}) custom-call(s32[32,64]{1,0:T(8,128)} %codes_ref.1, s32[1,512]{1,0:T(1,128)} %bitcast.4, f32[1,512]{1,0:T(1,128)} %bitcast.5, f32[1,512]{1,0:T(1,128)} %bitcast.6, f32[1,512]{1,0:T(1,128)} %bitcast.7, bf16[512,512]{1,0:T(8,128)(2,1)} %embed_hbm.1, ...), custom_call_target="tpu_custom_call" | custom-call | tf_op jit(solution)/shard_map/front/pallas_call | solution.py:508
  67.8 11.8 %back.1 = (f32[32,64,512]{2,1,0:T(8,128)}, f32[64,128,128]{2,1,0:T(8,128)}) custom-call(f32[32,64,512]{2,1,0:T(8,128)} %get-tuple-element.5.bo_in, f32[2048,128]{1,0:T(8,128)} %get-tuple-element.6.co_ref, f32[224,128]{1,0:T(8,128)} %get-tuple-element.7.halo_ref, bf16[3,3,128,128]{3,2,1,0:T(8,128)(2,1)} %k1_ref.1, bf16[3,3,128,128]{3,2,1,0:T(8,128)(2,1)} %k2_ref.1), custom_call_target="tpu_custom_call" | custom-call | tf_op jit(solution)/shard_map/back/pallas_call | solution.py:690

commit v7 on v6

--- a/solution.py
+++ b/solution.py
@@ -295,9 +295,9 @@
         kv_copy(k, 0, size, stage, sib).wait_recv()
 
     def relay(s):
-        k1 = s - 3
-
-        @pl.when((k1 >= 0) & (k1 < chunks))
+        k1 = jnp.where(s < 4, s - 2, s - 3)
+
+        @pl.when((k1 >= 0) & (k1 < chunks) & (s != 4))
         def _():
             arrived(k1, 0, 3)
             send(k1, beyond, 1, down)

time: 79.8 us -> 79.4 us (level)
  no operation moved by 1% of the time
where the time goes in v7:
time: 79.4 us; the launch traced here: 79.2 us
  Pallas kernels  78.5 us (99%)
    pallas_call x1, Pallas kernels, front_call(): pl.pallas_call(functools.partial(front_kernel, row_count, col_count), in_...  66.7 us
    pallas_call x1, Pallas kernels, back_call(): pl.pallas_call(back_kernel, grid=(2 * rows // fine_step,), in_specs=[anyw...  11.8 us

profile of v7, /device:TPU:3, one launch (start us, length us, event | category | flops | bytes accessed | tf_op | source)
XLA Modules:
  0.0 79.2 jit_solution(1233998027303625044)
XLA Ops:
  0.6 66.7 %front.1 = (f32[32,64,512]{2,1,0:T(8,128)}, f32[2048,128]{1,0:T(8,128)}, f32[224,128]{1,0:T(8,128)}) custom-call(s32[32,64]{1,0:T(8,128)} %codes_ref.1, s32[1,512]{1,0:T(1,128)} %bitcast.4, f32[1,512]{1,0:T(1,128)} %bitcast.5, f32[1,512]{1,0:T(1,128)} %bitcast.6, f32[1,512]{1,0:T(1,128)} %bitcast.7, bf16[512,512]{1,0:T(8,128)(2,1)} %embed_hbm.1, ...), custom_call_target="tpu_custom_call" | custom-call | tf_op jit(solution)/shard_map/front/pallas_call | solution.py:508
  67.4 11.8 %back.1 = (f32[32,64,512]{2,1,0:T(8,128)}, f32[64,128,128]{2,1,0:T(8,128)}) custom-call(f32[32,64,512]{2,1,0:T(8,128)} %get-tuple-element.5.bo_in, f32[2048,128]{1,0:T(8,128)} %get-tuple-element.6.co_ref, f32[224,128]{1,0:T(8,128)} %get-tuple-element.7.halo_ref, bf16[3,3,128,128]{3,2,1,0:T(8,128)(2,1)} %k1_ref.1, bf16[3,3,128,128]{3,2,1,0:T(8,128)(2,1)} %k2_ref.1), custom_call_target="tpu_custom_call" | custom-call | tf_op jit(solution)/shard_map/back/pallas_call | solution.py:690
